TPU v7x, 256 devices: a whole 4x4x8 slice. The times are simulated.
256 devices in a mesh: fsdp: 64 (over z, x_hi, y), seq: 4 (over x_lo, core).
Axes of the slice: x: 4 (x_hi: 2, x_lo: 2; x = x_hi * 2 + x_lo), y: 4, z: 8, core: 2. Of those that a mesh axis runs over, the one named last changes fastest.
Arguments:
- tokens: bfloat16 [64, 1500, 640], P('fsdp', 'seq'), may hold values from -6 to 6
- cotangent: bfloat16 [64, 1500, 640], P('fsdp', 'seq'), may hold values from -6 to 6
- codes_in: int32 [2560, 640], P(('fsdp', 'seq')), may hold values from 40 to 215, as said below
- scales_in: int32 [2560, 20], P(('fsdp', 'seq')), may hold values from 118 to 122
- codes_out: int32 [2560, 640], P(('fsdp', 'seq')), may hold values from 40 to 215, as said below
- scales_out: int32 [2560, 20], P(('fsdp', 'seq')), may hold values from 118 to 122
- layer_norm_gain: float32 [640], replicated, may hold values from 0.1 to 1.9
- layer_norm_bias: float32 [640], replicated, may hold values from -3 to 3
- bias_in: float32 [2560], replicated, may hold values from -3 to 3
- bias_out: float32 [640], replicated, may hold values from -3 to 3
- master_in: float32 [2560, 640], P(('fsdp', 'seq')), may hold values from -0.25 to 0.25
- moment_in: float32 [2560, 640], P(('fsdp', 'seq')), may hold values from -3 to 3
- second_in: float32 [2560, 640], P(('fsdp', 'seq')), may hold values from 0.01 to 1
- master_out: float32 [2560, 640], P(('fsdp', 'seq')), may hold values from -0.125 to 0.125
- moment_out: float32 [2560, 640], P(('fsdp', 'seq')), may hold values from -3 to 3
- second_out: float32 [2560, 640], P(('fsdp', 'seq')), may hold values from 0.01 to 1
Outputs:
- layer_out: bfloat16 [64, 1500, 640], P('fsdp', 'seq')
- d_tokens: bfloat16 [64, 1500, 640], P('fsdp', 'seq')
- d_gain: float32 [640], replicated
- d_shift: float32 [640], replicated
- d_bias_in: float32 [2560], replicated
- d_bias_out: float32 [640], replicated
- new_master_in: float32 [2560, 640], P(('fsdp', 'seq'))
- new_moment_in: float32 [2560, 640], P(('fsdp', 'seq'))
- new_second_in: float32 [2560, 640], P(('fsdp', 'seq'))
- new_master_out: float32 [2560, 640], P(('fsdp', 'seq'))
- new_moment_out: float32 [2560, 640], P(('fsdp', 'seq'))
- new_second_out: float32 [2560, 640], P(('fsdp', 'seq'))
Inputs may be any that keep to these rules, and one draw needn't show every extreme that they name: `codes_in`: each code is 128 times a sign bit plus 8 times an exponent field of 5 to 10 plus a mantissa of 0 to 7. `codes_out`: each code is 128 times a sign bit plus 8 times an exponent field of 5 to 10 plus a mantissa of 0 to 7.
All inputs are finite; a program needn't handle non-finite values.
Results may differ from a plain program's by a relative error of at most 0.013.
Values may be sent and summed in bfloat16 or wider, within the bound.
A program may use at most 128 MiB of HBM per device.

v0:
```python
import math

import jax
import jax.numpy as jnp
from jax import lax
from jax.sharding import PartitionSpec as P


def decode(codes, scales):
    sign_bit = (codes // 128).astype(jnp.float32)
    expo_field = codes // 8 % 16
    mant_field = (codes % 8).astype(jnp.float32)
    normal_mag = jnp.exp2(expo_field.astype(jnp.float32) - 7.0) * (1.0 + mant_field / 8.0)
    small_mag = mant_field * 2.0 ** (-9)
    values = (1.0 - 2.0 * sign_bit) * jnp.where(expo_field > 0, normal_mag, small_mag)
    blocks = jnp.exp2(scales.astype(jnp.float32) - 127.0)
    row_count, col_count = codes.shape
    scaled = values.reshape(row_count, col_count // 32, 32) * blocks[:, :, None]
    return scaled.reshape(row_count, col_count).astype(jnp.bfloat16)


def gelu_slope(values):
    return (
        0.5 * (1.0 + lax.erf(values * 0.7071067811865476))
        + values * jnp.exp(-0.5 * values * values) * 0.3989422804014327
    )


def contraction_rows(left, right):
    return lax.dot_general(
        left, right, (((0,), (0,)), ((), ())), preferred_element_type=jnp.float32
    )


def contract_cols(left, right):
    return lax.dot_general(
        left, right, (((1,), (1,)), ((), ())), preferred_element_type=jnp.float32
    )


def adamw(master, moment, second, grad):
    new_moment = 0.9 * moment + 0.1 * grad
    new_second = 0.95 * second + 0.05 * grad * grad
    new_master = master - 0.001 * (new_moment / (jnp.sqrt(new_second) + 1e-08) + 0.1 * master)
    return (new_master, new_moment, new_second)


def body(
    tokens,
    cotangent,
    codes_in,
    scales_in,
    codes_out,
    scales_out,
    layer_norm_gain,
    layer_norm_bias,
    bias_in,
    bias_out,
    master_in,
    moment_in,
    second_in,
    master_out,
    moment_out,
    second_out,
):
    clip_count, frame_count, width = tokens.shape
    row_count = clip_count * frame_count
    tok_rows = tokens.reshape(row_count, width)
    cotangent_rows = cotangent.reshape(row_count, width)
    piece_in = decode(codes_in, scales_in)
    piece_out = decode(codes_out, scales_out)
    w_in, w_out = (
        lax.all_gather(piece_in, ("fsdp", "seq"), axis=0, tiled=True),
        lax.all_gather(piece_out, ("fsdp", "seq"), axis=0, tiled=True),
    )
    tok_float = tok_rows.astype(jnp.float32)
    mean_removed = tok_float - jnp.mean(tok_float, axis=-1, keepdims=True)
    inverse_deviation = lax.rsqrt(
        jnp.mean(mean_removed * mean_removed, axis=-1, keepdims=True) + 1e-05
    )
    standardized_tokens = mean_removed * inverse_deviation
    normalized_tokens = (standardized_tokens * layer_norm_gain + layer_norm_bias).astype(
        jnp.bfloat16
    )
    pre = contract_cols(normalized_tokens, w_in) + bias_in
    gelu_output = jax.nn.gelu(pre, approximate=False).astype(jnp.bfloat16)
    layer = (
        tok_float + jnp.dot(gelu_output, w_out, preferred_element_type=jnp.float32) + bias_out
    ).astype(jnp.bfloat16)
    cotangent_float = cotangent_rows.astype(jnp.float32)
    preactivation_gradient = (contract_cols(cotangent_rows, w_out) * gelu_slope(pre)).astype(
        jnp.bfloat16
    )
    normalized_gradient = jnp.dot(preactivation_gradient, w_in, preferred_element_type=jnp.float32)
    standardized_gradient = normalized_gradient * layer_norm_gain
    token_gradient = (
        cotangent_float
        + inverse_deviation
        * (
            standardized_gradient
            - jnp.mean(standardized_gradient, axis=-1, keepdims=True)
            - standardized_tokens
            * jnp.mean(standardized_gradient * standardized_tokens, axis=-1, keepdims=True)
        )
    ).astype(jnp.bfloat16)
    fsdp_count = lax.axis_size("fsdp")
    seq_count = lax.axis_size("seq")
    reduction_factor = 1.0 / math.sqrt(fsdp_count * seq_count * row_count)
    d_gain, d_shift, d_bias_in, d_bias_out = lax.psum(
        (
            jnp.sum(normalized_gradient * standardized_tokens, axis=0) * reduction_factor,
            jnp.sum(normalized_gradient, axis=0) * reduction_factor,
            jnp.sum(preactivation_gradient.astype(jnp.float32), axis=0) * reduction_factor,
            jnp.sum(cotangent_float, axis=0) * reduction_factor,
        ),
        ("fsdp", "seq"),
    )
    columns = preactivation_gradient
    grad_in = lax.psum_scatter(
        contraction_rows(columns, normalized_tokens) * reduction_factor,
        ("fsdp", "seq"),
        scatter_dimension=0,
        tiled=True,
    )
    columns = gelu_output
    grad_out = lax.psum_scatter(
        contraction_rows(columns, cotangent_rows) * reduction_factor,
        ("fsdp", "seq"),
        scatter_dimension=0,
        tiled=True,
    )
    new_master_in, new_moment_in, new_second_in = adamw(master_in, moment_in, second_in, grad_in)
    new_master_out, new_moment_out, new_second_out = adamw(
        master_out, moment_out, second_out, grad_out
    )
    return (
        layer.reshape(tokens.shape),
        token_gradient.reshape(tokens.shape),
        d_gain,
        d_shift,
        d_bias_in,
        d_bias_out,
        new_master_in,
        new_moment_in,
        new_second_in,
        new_master_out,
        new_moment_out,
        new_second_out,
    )


def solution(mesh):
    placed = (
        P("fsdp", "seq", None),
        P("fsdp", "seq", None),
        P(("fsdp", "seq"), None),
        P(("fsdp", "seq"), None),
        P(("fsdp", "seq"), None),
        P(("fsdp", "seq"), None),
        P(),
        P(),
        P(),
        P(),
        P(("fsdp", "seq"), None),
        P(("fsdp", "seq"), None),
        P(("fsdp", "seq"), None),
        P(("fsdp", "seq"), None),
        P(("fsdp", "seq"), None),
        P(("fsdp", "seq"), None),
    )
    return jax.shard_map(
        body,
        mesh=mesh,
        in_specs=placed,
        out_specs=(
            P("fsdp", "seq", None),
            P("fsdp", "seq", None),
            P(),
            P(),
            P(),
            P(),
            P(("fsdp", "seq"), None),
            P(("fsdp", "seq"), None),
            P(("fsdp", "seq"), None),
            P(("fsdp", "seq"), None),
            P(("fsdp", "seq"), None),
            P(("fsdp", "seq"), None),
        ),
        check_vma=False,
    )
```

profile of v0, /device:TPU:8, one launch (start us, length us, event | category | flops | bytes accessed | tf_op | source)
XLA Modules:
  0.0 1167.0 jit_solution(12646621634016585647)
XLA Ops:
  7.2 0.0 all-gather.5.cloned.1.call-start
  7.2 0.7 multiply_exponential_fusion.1
  7.9 0.1 mul.199
  8.0 0.1 mul.200
  8.1 1.5 fusion.62
  9.6 0.0 all-gather.5.cloned.1.call-update
  9.6 0.0 all-gather.7.cloned.1.call-start
  9.7 0.7 multiply_exponential_fusion
  10.4 0.1 mul.209
  10.5 0.1 mul.210
  10.6 1.5 fusion.61
  12.1 0.0 all-gather.7.cloned.1.call-update
  12.1 0.0 all-reduce.6.cloned.1.call-start
  12.2 1.2 convert_reduce_fusion.2
  13.3 1.3 fusion.32
  14.7 0.0 copy-start.9
  14.7 412.5 %all-gather.5.cloned.1.call-done = bf16[256,10,640]{2,1,0:T(8,128)(2,1)} async-done(((bf16[1,10,640]{2,1,0:T(8,128)(2,1)}), bf16[256,10,640]{2,1,0:T(8,128)(2,1)}) %all-gather.5.cloned.1.call-update) | async-done | bytes 3276816 | tf_op jit(solution)/shard_map/all_gather | solution.py:73
  427.2 7.0 reshape.71
  434.3 12.0 %fusion.4 = (bf16[375,2560]{1,0:T(8,128)(2,1)S(1)}, f32[375,2560]{1,0:T(8,128)}) fusion(f32[2560]{0:T(1024)S(1)} %copy-done.11, bf16[2560,640]{1,0:T(8,128)(2,1)} %reshape.71, bf16[1,375,640]{2,1,0:T(8,128)(2,1)S(1)} %copy-done, f32[640]{0:T(1024)S(1)} %copy-done.10, f32[640]{0:T(1024)S(1)} %copy-done.9, f32[375]{0:T(512)S(1)} %add_rsqrt_fusion, ...), kind=kOutput, calls=%fused_computation.10 | convolution fusion | flops 1293600000 | bytes 9535160 | tf_op jit(solution)/shard_map/dot_general | solution.py:36
  446.3 398.7 %all-gather.7.cloned.1.call-done = bf16[256,10,640]{2,1,0:T(8,128)(2,1)} async-done(((bf16[1,10,640]{2,1,0:T(8,128)(2,1)}), bf16[256,10,640]{2,1,0:T(8,128)(2,1)}) %all-gather.7.cloned.1.call-update) | async-done | bytes 3276816 | tf_op jit(solution)/shard_map/all_gather | solution.py:74
  845.0 7.0 reshape.73
  852.0 6.3 convert_reduce_fusion
  858.3 4.9 convolution_multiply_fusion.1
  863.2 4.9 convolution_multiply_fusion
  868.1 0.0 all-reduce.6.cloned.1.call-update
  868.1 4.4 fusion.31
  872.5 1.2 convert_reduce_fusion.1
  873.8 78.1 %all-reduce.2 = (f32[640]{0:T(1024)}, f32[640]{0:T(1024)}, f32[2560]{0:T(1024)}, f32[640]{0:T(1024)}) all-reduce(f32[640]{0:T(1024)S(1)} %get-tuple-element.36, f32[640]{0:T(1024)S(1)} %get-tuple-element.35, f32[2560]{0:T(1024)S(1)} %broadcast_multiply_fusion, ...), channel_id=1, replica_groups=mesh['fsdp'=64,'seq'=4] {'fsdp','seq'}, use_global_device_ids=true, to_apply=%region_5.6 | all-reduce | flops 4480 | bytes 35840 | tf_op jit(solution)/shard_map/psum | solution.py:109
  951.8 0.0 copy-start.6
  951.9 4.6 fusion.18
  956.5 202.3 %all-reduce.6.cloned.1.call-done = (f32[2560,640]{1,0:T(8,128)}, f32[2560,640]{1,0:T(8,128)}) async-done(((f32[2560,640]{1,0:T(8,128)}, f32[2560,640]{1,0:T(8,128)}), (f32[2560,640]{1,0:T(8,128)}, f32[2560,640]{1,0:T(8,128)})) %all-reduce.6.cloned.1.call-update) | async-done | bytes 13107216
  1158.8 1.6 multiply_subtract_fusion
  (30 shorter events, 0.1 us)
Async XLA Ops:
  7.2 420.1 %all-gather.5.cloned.1.call-start = ((), (), s32[]{:S(2)}) async-start(), calls=%async_computation | async-start | bytes 5263360 | tf_op jit(solution)/shard_map/all_gather | solution.py:73
  9.6 835.3 %all-gather.7.cloned.1.call-start = ((), (), s32[]{:S(2)}) async-start(), calls=%async_computation.1 | async-start | bytes 5263360 | tf_op jit(solution)/shard_map/all_gather | solution.py:74
  12.1 1146.7 %all-reduce.6.cloned.1.call-start = ((), (), s32[]{:S(2)}) async-start(), calls=%async_computation.2 | async-start | bytes 26214400
  14.7 419.6 %copy-start = (bf16[1,375,640]{2,1,0:T(8,128)(2,1)S(1)}, bf16[1,375,640]{2,1,0:T(8,128)(2,1)}, u32[]{:S(2)}) copy-start(bf16[1,375,640]{2,1,0:T(8,128)(2,1)} %param.16) | copy-start | bytes 1440004
  14.7 419.6 %copy-start.9 = (f32[640]{0:T(1024)S(1)}, f32[640]{0:T(1024)}, u32[]{:S(2)}) copy-start(f32[640]{0:T(1024)} %param.22) | copy-start | bytes 7684
  14.7 419.6 %copy-start.10 = (f32[640]{0:T(1024)S(1)}, f32[640]{0:T(1024)}, u32[]{:S(2)}) copy-start(f32[640]{0:T(1024)} %param.23) | copy-start | bytes 7684
  14.7 419.6 %copy-start.11 = (f32[2560]{0:T(1024)S(1)}, f32[2560]{0:T(1024)}, u32[]{:S(2)}) copy-start(f32[2560]{0:T(1024)} %param.24) | copy-start | bytes 30724
  446.3 405.7 %copy-start.2 = (bf16[1,375,640]{2,1,0:T(8,128)(2,1)S(1)}, bf16[1,375,640]{2,1,0:T(8,128)(2,1)}, u32[]{:S(2)}) copy-start(bf16[1,375,640]{2,1,0:T(8,128)(2,1)} %param.17) | copy-start | bytes 1440004
  858.3 4.9 copy-start.1
  868.1 83.7 %copy-start.12 = (f32[640]{0:T(1024)S(1)}, f32[640]{0:T(1024)}, u32[]{:S(2)}) copy-start(f32[640]{0:T(1024)} %param.25) | copy-start | bytes 7684
  951.8 207.0 %copy-start.3 = (f32[10,640]{1,0:T(8,128)S(1)}, f32[10,640]{1,0:T(8,128)}, u32[]{:S(2)}) copy-start(f32[10,640]{1,0:T(8,128)} %param.29) | copy-start | bytes 76804
  951.8 207.0 %copy-start.4 = (f32[10,640]{1,0:T(8,128)S(1)}, f32[10,640]{1,0:T(8,128)}, u32[]{:S(2)}) copy-start(f32[10,640]{1,0:T(8,128)} %param.31) | copy-start | bytes 76804
  951.8 207.0 %copy-start.5 = (f32[10,640]{1,0:T(8,128)S(1)}, f32[10,640]{1,0:T(8,128)}, u32[]{:S(2)}) copy-start(f32[10,640]{1,0:T(8,128)} %param.30) | copy-start | bytes 76804
  951.8 207.0 %copy-start.6 = (f32[10,640]{1,0:T(8,128)S(1)}, f32[10,640]{1,0:T(8,128)}, u32[]{:S(2)}) copy-start(f32[10,640]{1,0:T(8,128)} %param.26) | copy-start | bytes 76804
  951.9 207.0 %copy-start.7 = (f32[10,640]{1,0:T(8,128)S(1)}, f32[10,640]{1,0:T(8,128)}, u32[]{:S(2)}) copy-start(f32[10,640]{1,0:T(8,128)} %param.28) | copy-start | bytes 76804
  951.9 207.0 %copy-start.8 = (f32[10,640]{1,0:T(8,128)S(1)}, f32[10,640]{1,0:T(8,128)}, u32[]{:S(2)}) copy-start(f32[10,640]{1,0:T(8,128)} %param.27) | copy-start | bytes 76804
Sparse Core Ops, SparseCore 0:
  10.5 416.7 all-gather.4
  429.7 415.2 all-gather.6
  868.2 290.5 all-reduce.5
where the time goes:
time: 1170 us
  waiting for transfers between devices  1010 us (86%)
  blocking collectives  78.1 us (7%)
  matrix products  37.1 us (3%)
  local copies, waits for them, and re-layouts  14.5 us (1%)
  between operations  13.9 us (1%)
    all_gather x1, waiting for transfers between devices, body(): lax.all_gather(piece_in, ('fsdp', 'seq'), axis=0, tiled=True)  413 us
    all_gather x1, waiting for transfers between devices, body(): lax.all_gather(piece_out, ('fsdp', 'seq'), axis=0, tiled=True)  399 us
    unnamed x4, waiting for transfers between devices  202 us
    psum x1, blocking collectives, body(): lax.psum((jnp.sum(normalized_gradient * standardized_tokens, axis=0) * re...  78.1 us
  transfers between devices with their start and end apart: 3, of which 3 were waited for; matrix products, arithmetic and copies ran while one was open for 3% of the time, Pallas kernels for 0%

commit v1 on v0

v1 whole, which is shorter than its diff:
```python
import math

import jax
import jax.numpy as jnp
from jax import lax
from jax.experimental import pallas as pl
from jax.experimental.pallas import tpu as pltpu
from jax.sharding import PartitionSpec as P

NX, NY, NZ, NC = 4, 4, 8, 2
WIDTH = 640
OWN = 10
FRAMES = 375
ROWS = 384
CHUNK = NZ * OWN
BLOCK = NX * CHUNK
HIDDEN = NY * BLOCK
SHARD = 32
TOKENS = 96000
BF, F32 = jnp.bfloat16, jnp.float32
MESH = pl.DeviceIdType.MESH


def dot_nn(a, b):
    return jnp.dot(a, b, preferred_element_type=F32)


def dot_nt(a, b):
    return lax.dot_general(a, b, (((1,), (1,)), ((), ())), preferred_element_type=F32)


def dot_tn(a, b):
    return lax.dot_general(a, b, (((0,), (0,)), ((), ())), preferred_element_type=F32)


def coordinates():
    f = lax.axis_index("fsdp")
    s = lax.axis_index("seq")
    y = lax.rem(f, 4)
    x_hi = lax.rem(f // 4, 2)
    return x_hi * 2 + s // 2, y, f // 8, lax.rem(s, 2)


def device(x, y, z, c):
    return ((z * 2 + x // 2) * 4 + y, lax.rem(x, 2) * 2 + c)


def decode(codes, scales):
    spread = (
        lax.broadcasted_iota(jnp.int32, (20, WIDTH), 1) // 32
        == lax.broadcasted_iota(jnp.int32, (20, WIDTH), 0)
    )
    k = dot_nn((scales - 118).astype(F32).astype(BF), spread.astype(F32).astype(BF)).astype(jnp.int32)
    negative = codes >= 128
    e = (codes >> 3) & 15
    m = codes & 7
    whole = jnp.where(e > 0, m + 8, m)
    value = (whole << (jnp.maximum(e, 1) + k - 1)).astype(F32) * (2.0**-18)
    return jnp.where(negative, -value, value)


def shard_select():
    r = lax.broadcasted_iota(jnp.int32, (2 * CHUNK, NZ * SHARD), 0)
    col = lax.broadcasted_iota(jnp.int32, (2 * CHUNK, NZ * SHARD), 1)
    second = (r >= CHUNK).astype(jnp.int32)
    r = r - CHUNK * second
    z = jnp.zeros_like(r)
    for j in range(1, NZ):
        z = z + (r >= OWN * j).astype(jnp.int32)
    return (col == z * (SHARD - OWN) + r + 16 * second).astype(F32).astype(BF)


def adamw(master, moment, second, grad):
    new_moment = 0.9 * moment + 0.1 * grad
    new_second = 0.95 * second + 0.05 * grad * grad
    new_master = master - 0.001 * (new_moment / (jnp.sqrt(new_second) + 1e-08) + 0.1 * master)
    return new_master, new_moment, new_second


def kernel(
    tok_ref, cot_ref, cin_ref, sin_ref, cout_ref, sout_ref,
    gain_ref, shift_ref, bin_ref, bout_ref,
    min_ref, vin_ref, qin_ref, mout_ref, vout_ref, qout_ref,
    layer_ref, dtok_ref, vec_ref,
    omin_ref, ovin_ref, oqin_ref, omout_ref, ovout_ref, oqout_ref,
    tokb, cotb, normed, xhat, rstd, shard, zbuf, win, wout, bcol, dbp, act, dpre,
    gin, gout, r1in, r1out, s1in, s1out, r2in, r2out, zsend, r3,
    part, partr, vown, vcore, vy, vx, vz,
    cs, cr, zs, zr, a2s, a2r, a3s, a3r, g1is, g1ir, g1os, g1or, g2s, g2r, g3s, g3r, ps, pr, vs, vr,
):
    x, y, z, c = coordinates()
    xp = [lax.rem(x + d, NX) for d in range(NX)]
    yp = [lax.rem(y + d, NY) for d in range(NY)]
    zp = [lax.rem(z + d, NZ) for d in range(NZ)]
    to_x = [device(q, y, z, c) for q in xp]
    to_y = [device(x, q, z, c) for q in yp]
    to_z = [device(x, y, q, c) for q in zp]
    to_c = device(x, y, z, 1 - c)
    pending = []

    def send(src, dst, ssem, rsem, target):
        copy = pltpu.make_async_remote_copy(
            src_ref=src, dst_ref=dst, send_sem=ssem, recv_sem=rsem,
            device_id=target, device_id_type=MESH,
        )
        copy.start()
        pending.append(copy)
        return copy

    barrier = pltpu.get_barrier_semaphore()
    for q in to_x[1:] + to_y[1:] + to_z[1:] + [to_c]:
        pl.semaphore_signal(barrier, inc=1, device_id=q, device_id_type=MESH)

    shard[...] = jnp.zeros_like(shard)
    shard[0:OWN, :] = decode(cin_ref[...], sin_ref[...]).astype(BF)
    shard[16 : 16 + OWN, :] = decode(cout_ref[...], sout_ref[...]).astype(BF)
    zbuf[z] = shard[...]
    for buf, ref in ((tokb, tok_ref), (cotb, cot_ref)):
        buf[ROWS - 16 : ROWS, :] = jnp.zeros((16, WIDTH), BF)
        buf[0:FRAMES, :] = ref[0]
    pl.semaphore_wait(barrier, NX + NY + NZ - 2)

    zc = [
        send(shard, zbuf.at[z], zs.at[d - 1], zr.at[d - 1], to_z[d])
        for d in (4, 3, 5, 2, 6, 1, 7)
    ]
    own, other = slice(0, ROWS), slice(ROWS, 2 * ROWS)
    cc = [
        send(buf.at[own], buf.at[other], cs.at[i], cr.at[i], to_c)
        for i, buf in enumerate((tokb, cotb))
    ]

    def norm(rows):
        t = tokb[rows, :].astype(F32)
        t = t - jnp.mean(t, axis=-1, keepdims=True)
        inv = lax.rsqrt(jnp.mean(t * t, axis=-1, keepdims=True) + 1e-05)
        t = t * inv
        normed[rows, :] = (t * gain_ref[...] + shift_ref[...]).astype(BF)
        return t, inv

    t, inv = norm(own)
    xhat[...] = t
    rstd[...] = inv
    bias = jnp.where(c == 0, bin_ref[0:1, :], bin_ref[1:2, :])
    bcol[...] = jnp.transpose(jnp.broadcast_to(bias, (128, HIDDEN)))
    select = shard_select()
    for copy in cc:
        copy.wait_recv()
    norm(other)

    for copy in zc:
        copy.wait_recv()
    w = dot_nn(select, zbuf[...].reshape(NZ * SHARD, WIDTH)).astype(BF)
    win[y, x] = w[:CHUNK]
    wout[y, x] = w[CHUNK:]

    def second(d):
        return (
            send(win.at[y, x], win.at[y, x], a2s.at[0, d - 1], a2r.at[0, d - 1], to_x[d]),
            send(wout.at[y, x], wout.at[y, x], a2s.at[1, d - 1], a2r.at[1, d - 1], to_y[d]),
        )

    def third(d):
        fx, fy = lax.rem(x + NX - d, NX), lax.rem(y + NY - d, NY)
        out = []
        for e in (1, 3, 2):
            out.append(send(win.at[y, fx], win.at[y, fx], a3s.at[0, d, e - 1], a3r.at[0, d, e - 1], to_y[e]))
            out.append(send(wout.at[fy, x], wout.at[fy, x], a3s.at[1, d, e - 1], a3r.at[1, d, e - 1], to_x[e]))
        return out

    c2 = {d: second(d) for d in (1, 3, 2)}
    c3 = third(0)
    for d in (1, 3, 2):
        for copy in c2[d]:
            copy.wait_recv()
        c3 += third(d)
    for copy in c3:
        copy.wait_recv()

    g1i, g1o = [], []
    for d in (1, 3, 2, 0):
        by = yp[d]
        rows = pl.ds(pl.multiple_of(by * BLOCK, BLOCK), BLOCK)
        v = dot_nt(win[by].reshape(BLOCK, WIDTH), normed[...]) + bcol[rows, 0:1]
        phi = 0.5 * (1.0 + lax.erf(v * 0.7071067811865476))
        slope = phi + v * jnp.exp(-0.5 * v * v) * 0.3989422804014327
        a = (v * phi).astype(BF)
        act[rows, :] = a
        dp = dot_nt(wout[by].reshape(BLOCK, WIDTH), cotb[...]) * slope
        folded = dp[:, 0:128]
        for j in range(1, 6):
            folded = folded + dp[:, 128 * j : 128 * j + 128]
        dbp[rows, :] = folded
        dp = dp.astype(BF)
        dpre[rows, :] = dp
        gin[by] = dot_nn(dp, normed[...]).astype(BF).reshape(NX, CHUNK, WIDTH)
        if d:
            g1i.append(send(gin.at[by], r1in.at[d - 1], g1is.at[d - 1], g1ir.at[d - 1], to_y[d]))
        gout[by] = dot_nn(a, cotb[...]).astype(BF).reshape(NX, CHUNK, WIDTH)
        for e in (1, 3, 2):
            g1o.append(
                send(gout.at[by, xp[e]], r1out.at[e - 1, by], g1os.at[d, e - 1], g1or.at[d, e - 1], to_x[e])
            )

    wi = win[...].reshape(HIDDEN, WIDTH)
    wo = wout[...].reshape(HIDDEN, WIDTH)
    pc = []
    part[0, 1] = dot_tn(act[:, other], wo)
    pc.append(send(part.at[0, 1], partr.at[0], ps.at[0], pr.at[0], to_c))
    part[1, 1] = dot_tn(dpre[:, other], wi)
    pc.append(send(part.at[1, 1], partr.at[1], ps.at[1], pr.at[1], to_c))
    part[0, 0] = dot_tn(act[:, own], wo)
    part[1, 0] = dot_tn(dpre[:, own], wi)
    cot = cotb[own, :].astype(F32)
    pc[0].wait_recv()
    layer = tokb[own, :].astype(F32) + (part[0, 0] + partr[0]) + bout_ref[...]
    layer_ref[0] = layer.astype(BF)[0:FRAMES]
    pc[1].wait_recv()
    dn = part[1, 0] + partr[1]
    xh = xhat[...]
    dx = dn * gain_ref[...]
    dt = cot + rstd[...] * (
        dx - jnp.mean(dx, axis=-1, keepdims=True) - xh * jnp.mean(dx * xh, axis=-1, keepdims=True)
    )
    dtok_ref[0] = dt.astype(BF)[0:FRAMES]

    db = jnp.sum(jnp.transpose(dbp[...]), axis=0, keepdims=True)
    zero = jnp.zeros_like(db)
    db0, db1 = jnp.where(c == 0, db, zero), jnp.where(c == 0, zero, db)
    vown[0:1, :] = db0[:, 0:WIDTH]
    vown[1:2, :] = db0[:, WIDTH:]
    vown[2:3, :] = db1[:, 0:WIDTH]
    vown[3:4, :] = db1[:, WIDTH:]
    vown[4:5, :] = jnp.sum(dn * xh, axis=0, keepdims=True)
    vown[5:6, :] = jnp.sum(dn, axis=0, keepdims=True)
    vown[6:7, :] = jnp.sum(cot, axis=0, keepdims=True)
    vown[7:8, :] = jnp.zeros((1, WIDTH), F32)
    vc = send(vown, vcore, vs.at[0], vr.at[0], to_c)
    vc.wait_recv()
    vy[y] = vown[...] + vcore[...]
    vyc = [send(vy.at[y], vy.at[y], vs.at[d], vr.at[d], to_y[d]) for d in (1, 3, 2)]

    def add_in():
        for copy in g1i:
            copy.wait_recv()
        for q in range(NX):
            total = gin[y, q].astype(F32)
            for d in range(3):
                total = total + r1in[d, q].astype(F32)
            s1in[q] = total.astype(BF)

    def add_out():
        for copy in g1o:
            copy.wait_recv()
        for q in range(NY):
            total = gout[q, x].astype(F32)
            for d in range(3):
                total = total + r1out[d, q].astype(F32)
            s1out[q] = total.astype(BF)

    add_in()
    g2 = [send(s1in.at[xp[d]], r2in.at[d - 1], g2s.at[0, d - 1], g2r.at[0, d - 1], to_x[d]) for d in (1, 3, 2)]
    add_out()
    g2 += [send(s1out.at[yp[d]], r2out.at[d - 1], g2s.at[1, d - 1], g2r.at[1, d - 1], to_y[d]) for d in (1, 3, 2)]
    for copy in vyc:
        copy.wait_recv()
    vx[x] = (vy[0] + vy[1]) + (vy[2] + vy[3])
    vxc = [send(vx.at[x], vx.at[x], vs.at[3 + d], vr.at[3 + d], to_x[d]) for d in (1, 3, 2)]

    for copy in g2:
        copy.wait_recv()
    sums = []
    for first, got in ((s1in[x], r2in), (s1out[y], r2out)):
        total = first.astype(F32)
        for d in range(3):
            total = total + got[d].astype(F32)
        sums.append(total.astype(BF))
    both = jnp.concatenate(sums, axis=0)
    zsend[...] = dot_tn(select, both).astype(BF).reshape(NZ, SHARD, WIDTH)
    g3 = [
        send(zsend.at[zp[d]], r3.at[d - 1], g3s.at[d - 1], g3r.at[d - 1], to_z[d])
        for d in (4, 3, 5, 2, 6, 1, 7)
    ]
    for copy in vxc:
        copy.wait_recv()
    vz[z] = (vx[0] + vx[1]) + (vx[2] + vx[3])
    vzc = [send(vz.at[z], vz.at[z], vs.at[6 + d], vr.at[6 + d], to_z[d]) for d in (4, 3, 5, 2, 6, 1, 7)]

    for copy in g3:
        copy.wait_recv()
    grad = zsend[z].astype(F32)
    for d in range(NZ - 1):
        grad = grad + r3[d].astype(F32)
    grad = grad * (1.0 / math.sqrt(TOKENS))
    omin_ref[...], ovin_ref[...], oqin_ref[...] = adamw(
        min_ref[...], vin_ref[...], qin_ref[...], grad[0:OWN]
    )
    omout_ref[...], ovout_ref[...], oqout_ref[...] = adamw(
        mout_ref[...], vout_ref[...], qout_ref[...], grad[16 : 16 + OWN]
    )
    for copy in vzc:
        copy.wait_recv()
    total = vz[0]
    for q in range(1, NZ):
        total = total + vz[q]
    vec_ref[...] = total * (1.0 / math.sqrt(TOKENS))
    for copy in pending:
        copy.wait_send()


def body(
    tokens, cotangent, codes_in, scales_in, codes_out, scales_out,
    layer_norm_gain, layer_norm_bias, bias_in, bias_out,
    master_in, moment_in, second_in, master_out, moment_out, second_out,
):
    bias = bias_in.reshape(NZ, 2, NY, 2, NC, OWN).transpose(4, 2, 1, 3, 0, 5).reshape(NC, HIDDEN)
    vmem = pl.BlockSpec(memory_space=pltpu.VMEM)
    owned = jax.ShapeDtypeStruct((OWN, WIDTH), F32)
    dma = pltpu.SemaphoreType.DMA
    outs = pl.pallas_call(
        kernel,
        out_shape=[
            jax.ShapeDtypeStruct(tokens.shape, BF),
            jax.ShapeDtypeStruct(tokens.shape, BF),
            jax.ShapeDtypeStruct((8, WIDTH), F32),
        ]
        + [owned] * 6,
        in_specs=[vmem] * 16,
        out_specs=[vmem] * 9,
        scratch_shapes=[
            pltpu.VMEM((2 * ROWS, WIDTH), BF),
            pltpu.VMEM((2 * ROWS, WIDTH), BF),
            pltpu.VMEM((2 * ROWS, WIDTH), BF),
            pltpu.VMEM((ROWS, WIDTH), F32),
            pltpu.VMEM((ROWS, 1), F32),
            pltpu.VMEM((SHARD, WIDTH), BF),
            pltpu.VMEM((NZ, SHARD, WIDTH), BF),
            pltpu.VMEM((NY, NX, CHUNK, WIDTH), BF),
            pltpu.VMEM((NY, NX, CHUNK, WIDTH), BF),
            pltpu.VMEM((HIDDEN, 128), F32),
            pltpu.VMEM((HIDDEN, 128), F32),
            pltpu.VMEM((HIDDEN, 2 * ROWS), BF),
            pltpu.VMEM((HIDDEN, 2 * ROWS), BF),
            pltpu.VMEM((NY, NX, CHUNK, WIDTH), BF),
            pltpu.VMEM((NY, NX, CHUNK, WIDTH), BF),
            pltpu.VMEM((NY - 1, NX, CHUNK, WIDTH), BF),
            pltpu.VMEM((NX - 1, NY, CHUNK, WIDTH), BF),
            pltpu.VMEM((NX, CHUNK, WIDTH), BF),
            pltpu.VMEM((NY, CHUNK, WIDTH), BF),
            pltpu.VMEM((NX - 1, CHUNK, WIDTH), BF),
            pltpu.VMEM((NY - 1, CHUNK, WIDTH), BF),
            pltpu.VMEM((NZ, SHARD, WIDTH), BF),
            pltpu.VMEM((NZ - 1, SHARD, WIDTH), BF),
            pltpu.VMEM((2, 2, ROWS, WIDTH), F32),
            pltpu.VMEM((2, ROWS, WIDTH), F32),
            pltpu.VMEM((8, WIDTH), F32),
            pltpu.VMEM((8, WIDTH), F32),
            pltpu.VMEM((NY, 8, WIDTH), F32),
            pltpu.VMEM((NX, 8, WIDTH), F32),
            pltpu.VMEM((NZ, 8, WIDTH), F32),
            dma((2,)), dma((2,)),
            dma((7,)), dma((7,)),
            dma((2, 3)), dma((2, 3)),
            dma((2, 4, 3)), dma((2, 4, 3)),
            dma((3,)), dma((3,)),
            dma((4, 3)), dma((4, 3)),
            dma((2, 3)), dma((2, 3)),
            dma((7,)), dma((7,)),
            dma((2,)), dma((2,)),
            dma((14,)), dma((14,)),
        ],
        compiler_params=pltpu.CompilerParams(
            collective_id=0, has_side_effects=True, vmem_limit_bytes=56 * 2**20
        ),
    )(
        tokens, cotangent, codes_in, scales_in, codes_out, scales_out,
        layer_norm_gain.reshape(1, WIDTH), layer_norm_bias.reshape(1, WIDTH),
        bias, bias_out.reshape(1, WIDTH),
        master_in, moment_in, second_in, master_out, moment_out, second_out,
    )
    layer, d_tokens, vec = outs[:3]
    d_bias_in = (
        vec[0:4].reshape(NC, NY, 2, 2, NZ, OWN).transpose(4, 2, 1, 3, 0, 5).reshape(NC * HIDDEN)
    )
    return (layer, d_tokens, vec[4], vec[5], d_bias_in, vec[6]) + tuple(outs[3:])


def solution(mesh):
    tokens, rows, whole = P("fsdp", "seq", None), P(("fsdp", "seq"), None), P()
    return jax.shard_map(
        body,
        mesh=mesh,
        in_specs=(tokens,) * 2 + (rows,) * 4 + (whole,) * 4 + (rows,) * 6,
        out_specs=(tokens,) * 2 + (whole,) * 4 + (rows,) * 6,
        check_vma=False,
    )
```

time: 1170 us -> 101 us (0.09)
  waiting for transfers between devices: 1010 us -> 0 us
  Pallas kernels: 0 us -> 86 us
  blocking collectives: 78.1 us -> 0 us
  matrix products: 37.1 us -> 0 us
  between operations: 13.9 us -> 0.72 us
    all_gather x2 -> x0, waiting for transfers between devices: 811 us -> none  [the longest x1 413 us: body(): lax.all_gather(piece_in, ('fsdp', 'seq'), axis=0, tiled=True)]
    unnamed x4 -> x0, waiting for transfers between devices: 202 us -> none
    pallas_call x0 -> x1, Pallas kernels: none -> 86 us  [body(): pl.pallas_call(kernel, out_shape=[jax.ShapeDtypeStruct(tokens.shape, BF),...]
    psum x1 -> x0, blocking collectives: 78.1 us -> none  [body(): lax.psum((jnp.sum(normalized_gradient * standardized_tokens, axis=0) * re...]
    dot_general x6 -> x0, matrix products: 37.1 us -> none  [the longest x2 18.3 us: contract_cols(): lax.dot_general(left, right, (((1,), (1,)), ((), ())), preferred_element_...]
  transfers between devices with their start and end apart: 3 -> 0, of which waited for: 3 -> 0; matrix products, arithmetic and copies ran while one was open for 3% -> 0% of each run, Pallas kernels for 0% -> 0%
where the time goes in v1:
time: 101 us
  Pallas kernels  86 us (85%)
  local copies, waits for them, and re-layouts  14 us (14%)
    pallas_call x1, Pallas kernels, body(): pl.pallas_call(kernel, out_shape=[jax.ShapeDtypeStruct(tokens.shape, BF),...  86 us
    unnamed x28, local copies, waits for them, and re-layouts  6.57 us

profile of v1, /device:TPU:8, one launch (start us, length us, event | category | flops | bytes accessed | tf_op | source)
XLA Modules:
  0.0 100.7 jit_solution(13033878228477300882)
XLA Ops:
  0.6 0.0 copy-start.8
  0.7 1.3 %reshape.45.gain_ref = f32[1,640]{1,0:T(1,128)} reshape(f32[640]{0:T(1024)} %param.22) | data formatting | bytes 5120 | tf_op jit(solution)/shard_map/reshape | solution.py:377
  1.9 1.3 %reshape.46.shift_ref = f32[1,640]{1,0:T(1,128)} reshape(f32[640]{0:T(1024)} %param.23) | data formatting | bytes 5120 | tf_op jit(solution)/shard_map/reshape | solution.py:377
  3.2 0.2 reshape.47
  3.4 0.1 copy.28
  3.5 0.0 copy-start.9
  3.5 0.7 reshape.48.bin_ref
  4.3 0.0 copy-done.9
  4.3 0.6 reshape.49.bout_ref
  4.8 86.0 %shard_map.247 = (bf16[1,375,640]{2,1,0:T(8,128)(2,1)}, bf16[1,375,640]{2,1,0:T(8,128)(2,1)}, f32[8,640]{1,0:T(8,128)}, f32[10,640]{1,0:T(8,128)}, f32[10,640]{1...) custom-call(bf16[1,375,640]{2,1,0:T(8,128)(2,1)} %tok_ref.1, ...), custom_call_target="tpu_custom_call" | custom-call | tf_op jit(solution)/shard_map/pallas_call | solution.py:320
  90.8 0.0 copy-start.1
  90.8 1.5 %slice_reduce_fusion = (f32[640]{0:T(1024)}, f32[640]{0:T(1024)}, f32[640]{0:T(1024)}) fusion(f32[8,640]{1,0:T(8,128)} %get-tuple-element.23), kind=kLoop, calls=%fused_computation.1 | loop fusion | bytes 15360 | tf_op jit(solution)/shard_map/slice | solution.py:385
  92.3 0.7 slice.14
  93.0 0.1 reshape.50
  93.2 0.1 copy.31
  93.3 0.8 reshape.51
  94.1 0.0 copy-done.1
  94.1 0.8 copy.40
  94.9 0.4 copy-done
  95.3 0.8 copy.41
  96.1 0.0 copy-done.7
  96.1 0.6 copy.42
  96.7 0.2 copy-done.6
  96.9 0.6 copy.43
  97.5 0.2 copy-done.5
  97.7 0.6 copy.44
  98.3 0.2 copy-done.4
  98.5 0.6 copy.45
  99.1 0.2 copy-done.3
  99.3 0.6 copy.46
  99.9 0.2 copy-done.2
  100.1 0.6 copy.47
  (8 shorter events, 0.0 us)
Async XLA Ops:
  0.6 2.6 %copy-start.8 = (f32[2560]{0:T(1024)S(1)}, f32[2560]{0:T(1024)}, u32[]{:S(2)}) copy-start(f32[2560]{0:T(1024)} %param.24) | copy-start | bytes 30724
  3.5 0.8 copy-start.9
  90.8 3.3 %copy-start.1 = (bf16[1,375,640]{2,1,0:T(8,128)(2,1)S(1)}, bf16[1,375,640]{2,1,0:T(8,128)(2,1)}, u32[]{:S(2)}) copy-start(bf16[1,375,640]{2,1,0:T(8,128)(2,1)} %get-tuple-element.45) | copy-start | bytes 1440004
  94.1 1.2 %copy-start = (bf16[1,375,640]{2,1,0:T(8,128)(2,1)S(1)}, bf16[1,375,640]{2,1,0:T(8,128)(2,1)}, u32[]{:S(2)}) copy-start(bf16[1,375,640]{2,1,0:T(8,128)(2,1)} %get-tuple-element.46) | copy-start | bytes 1440004
  95.3 0.8 copy-start.7
  96.1 0.8 copy-start.6
  96.9 0.8 copy-start.5
  97.7 0.8 copy-start.4
  98.5 0.8 copy-start.3
  99.3 0.8 copy-start.2

commit v2 on v1

--- a/solution.py
+++ b/solution.py
@@ -70,6 +70,24 @@
     return (col == z * (SHARD - OWN) + r + 16 * second).astype(F32).astype(BF)
 
 
+def order_mask():
+    j = lax.broadcasted_iota(jnp.int32, (128, WIDTH), 1)
+    later = (j >= 320).astype(jnp.int32)
+    j = j - 320 * later
+    group = (j * 6554) >> 16
+    return group, later * OWN + j - OWN * group
+
+
+def group_of(xx, yy, c):
+    return ((xx // 2 * 4 + yy) * 2 + xx % 2) * 2 + c
+
+
+def dot_exact(a, b, dims):
+    return lax.dot_general(
+        a, b, (dims, ((), ())), preferred_element_type=F32, precision=lax.Precision.HIGHEST
+    )
+
+
 def adamw(master, moment, second, grad):
     new_moment = 0.9 * moment + 0.1 * grad
     new_second = 0.95 * second + 0.05 * grad * grad
@@ -80,13 +98,11 @@
 def kernel(
     tok_ref, cot_ref, cin_ref, sin_ref, cout_ref, sout_ref,
     gain_ref, shift_ref, bin_ref, bout_ref,
-    min_ref, vin_ref, qin_ref, mout_ref, vout_ref, qout_ref,
-    layer_ref, dtok_ref, vec_ref,
-    omin_ref, ovin_ref, oqin_ref, omout_ref, ovout_ref, oqout_ref,
+    layer_ref, dtok_ref, vec_ref, grad_ref,
     tokb, cotb, normed, xhat, rstd, shard, zbuf, win, wout, bcol, dbp, act, dpre,
     gin, gout, r1in, r1out, s1in, s1out, r2in, r2out, zsend, r3,
     part, partr, vown, vcore, vy, vx, vz,
-    cs, cr, zs, zr, a2s, a2r, a3s, a3r, g1is, g1ir, g1os, g1or, g2s, g2r, g3s, g3r, ps, pr, vs, vr,
+    cs, cr, zs, zr, ws, wr, g1is, g1ir, g1os, g1or, g2s, g2r, g3s, g3r, ps, pr, vs, vr,
 ):
     x, y, z, c = coordinates()
     xp = [lax.rem(x + d, NX) for d in range(NX)]
@@ -130,19 +146,33 @@
         for i, buf in enumerate((tokb, cotb))
     ]
 
+    gain, shift = gain_ref[...].reshape(1, WIDTH), shift_ref[...].reshape(1, WIDTH)
+
     def norm(rows):
         t = tokb[rows, :].astype(F32)
         t = t - jnp.mean(t, axis=-1, keepdims=True)
         inv = lax.rsqrt(jnp.mean(t * t, axis=-1, keepdims=True) + 1e-05)
         t = t * inv
-        normed[rows, :] = (t * gain_ref[...] + shift_ref[...]).astype(BF)
+        normed[rows, :] = (t * gain + shift).astype(BF)
         return t, inv
 
     t, inv = norm(own)
     xhat[...] = t
     rstd[...] = inv
-    bias = jnp.where(c == 0, bin_ref[0:1, :], bin_ref[1:2, :])
-    bcol[...] = jnp.transpose(jnp.broadcast_to(bias, (128, HIDDEN)))
+    group, place = order_mask()
+    row = lax.broadcasted_iota(jnp.int32, (128, WIDTH), 0)
+    in_group = row == group
+    hot = [(row == place + 2 * OWN * p).astype(F32) for p in range(4)]
+    bias = jnp.zeros((128, 128), F32)
+    for p in range(4):
+        line = bin_ref[pl.ds(p * WIDTH, WIDTH)].reshape(1, WIDTH)
+        bias = bias + dot_exact(hot[p], jnp.where(in_group, line, 0.0), ((1,), (1,)))
+    for yy in range(NY):
+        for xx in range(NX):
+            g = group_of(xx, yy, 0)
+            bcol[(yy * NX + xx) * CHUNK : (yy * NX + xx + 1) * CHUNK, :] = jnp.where(
+                c == 0, bias[:CHUNK, g : g + 1], bias[:CHUNK, g + 1 : g + 2]
+            )
     select = shard_select()
     for copy in cc:
         copy.wait_recv()
@@ -154,34 +184,63 @@
     win[y, x] = w[:CHUNK]
     wout[y, x] = w[CHUNK:]
 
-    def second(d):
-        return (
-            send(win.at[y, x], win.at[y, x], a2s.at[0, d - 1], a2r.at[0, d - 1], to_x[d]),
-            send(wout.at[y, x], wout.at[y, x], a2s.at[1, d - 1], a2r.at[1, d - 1], to_y[d]),
-        )
-
-    def third(d):
-        fx, fy = lax.rem(x + NX - d, NX), lax.rem(y + NY - d, NY)
-        out = []
-        for e in (1, 3, 2):
-            out.append(send(win.at[y, fx], win.at[y, fx], a3s.at[0, d, e - 1], a3r.at[0, d, e - 1], to_y[e]))
-            out.append(send(wout.at[fy, x], wout.at[fy, x], a3s.at[1, d, e - 1], a3r.at[1, d, e - 1], to_x[e]))
-        return out
-
-    c2 = {d: second(d) for d in (1, 3, 2)}
-    c3 = third(0)
-    for d in (1, 3, 2):
-        for copy in c2[d]:
-            copy.wait_recv()
-        c3 += third(d)
-    for copy in c3:
-        copy.wait_recv()
-
-    g1i, g1o = [], []
-    for d in (1, 3, 2, 0):
+    to = ((to_x[1], to_x[3]), (to_y[1], to_y[3]))
+
+    class Item:
+        def __init__(self, index, axis, slot, half):
+            self.index, self.axis, self.half = index, axis, half
+            self.at = [slot(d) for d in range(4)]
+            self.copies = [None] * 4
+
+        def go(self, k, ref):
+            self.copies[k] = send(ref, ref, ws.at[self.index, k], wr.at[self.index, k], to[self.axis][k % 2])
+
+        def start(self):
+            self.go(0, self.at[0])
+            self.go(1, self.at[0])
+
+        def forward(self, k):
+            self.copies[k].wait_recv()
+            if k == 0:
+                self.go(2, self.at[3].at[0 : self.half])
+            else:
+                self.go(3, self.at[1].at[self.half : CHUNK])
+
+        def finish(self):
+            self.copies[2].wait_recv()
+            self.copies[3].wait_recv()
+
+    first_in = Item(0, 0, lambda d: win.at[y, xp[d]], 48)
+    first_out = Item(1, 1, lambda d: wout.at[yp[d], x], 48)
+    later_in = [Item(2 + p, 1, lambda d, p=p: win.at[yp[d], xp[p]], (32, 48)[p % 2]) for p in range(4)]
+    later_out = [Item(6 + p, 0, lambda d, p=p: wout.at[yp[p], xp[d]], (32, 48)[p % 2]) for p in range(4)]
+    first_in.start()
+    first_out.start()
+    later_in[0].start()
+    later_out[0].start()
+    for k, p in ((0, 3), (1, 1)):
+        first_in.forward(k)
+        first_out.forward(k)
+        later_in[p].start()
+        later_out[p].start()
+    for k in (0, 1):
+        later_in[0].forward(k)
+        later_out[0].forward(k)
+    first_in.finish()
+    first_out.finish()
+    later_in[2].start()
+    later_out[2].start()
+    for p in (3, 1):
+        for k in (0, 1):
+            later_in[p].forward(k)
+            later_out[p].forward(k)
+
+    g1i, g1o = [], {}
+
+    def block(d):
         by = yp[d]
         rows = pl.ds(pl.multiple_of(by * BLOCK, BLOCK), BLOCK)
-        v = dot_nt(win[by].reshape(BLOCK, WIDTH), normed[...]) + bcol[rows, 0:1]
+        v = dot_nt(win[by].reshape(BLOCK, WIDTH), normed[...]) + bcol[rows, :]
         phi = 0.5 * (1.0 + lax.erf(v * 0.7071067811865476))
         slope = phi + v * jnp.exp(-0.5 * v * v) * 0.3989422804014327
         a = (v * phi).astype(BF)
@@ -194,13 +253,32 @@
         dp = dp.astype(BF)
         dpre[rows, :] = dp
         gin[by] = dot_nn(dp, normed[...]).astype(BF).reshape(NX, CHUNK, WIDTH)
+        gout[by] = dot_nn(a, cotb[...]).astype(BF).reshape(NX, CHUNK, WIDTH)
+
+    def block_send(d):
+        by = yp[d]
         if d:
             g1i.append(send(gin.at[by], r1in.at[d - 1], g1is.at[d - 1], g1ir.at[d - 1], to_y[d]))
-        gout[by] = dot_nn(a, cotb[...]).astype(BF).reshape(NX, CHUNK, WIDTH)
-        for e in (1, 3, 2):
-            g1o.append(
-                send(gout.at[by, xp[e]], r1out.at[e - 1, by], g1os.at[d, e - 1], g1or.at[d, e - 1], to_x[e])
-            )
+        g1o[d] = [
+            send(gout.at[by, xp[e]], r1out.at[e - 1, by], g1os.at[d, e - 1], g1or.at[d, e - 1], to_x[e])
+            for e in (2, 1, 3)
+        ]
+
+    later_out[0].finish()
+    block(0)
+    for k in (0, 1):
+        later_in[2].forward(k)
+        later_out[2].forward(k)
+    block_send(0)
+    for p in (1, 3):
+        later_out[p].finish()
+        block(p)
+        block_send(p)
+    later_out[2].finish()
+    for p in range(4):
+        later_in[p].finish()
+    block(2)
+    block_send(2)
 
     wi = win[...].reshape(HIDDEN, WIDTH)
     wo = wout[...].reshape(HIDDEN, WIDTH)
@@ -213,24 +291,27 @@
     part[1, 0] = dot_tn(dpre[:, own], wi)
     cot = cotb[own, :].astype(F32)
     pc[0].wait_recv()
-    layer = tokb[own, :].astype(F32) + (part[0, 0] + partr[0]) + bout_ref[...]
+    layer = tokb[own, :].astype(F32) + (part[0, 0] + partr[0]) + bout_ref[...].reshape(1, WIDTH)
     layer_ref[0] = layer.astype(BF)[0:FRAMES]
     pc[1].wait_recv()
     dn = part[1, 0] + partr[1]
     xh = xhat[...]
-    dx = dn * gain_ref[...]
+    dx = dn * gain
     dt = cot + rstd[...] * (
         dx - jnp.mean(dx, axis=-1, keepdims=True) - xh * jnp.mean(dx * xh, axis=-1, keepdims=True)
     )
     dtok_ref[0] = dt.astype(BF)[0:FRAMES]
 
-    db = jnp.sum(jnp.transpose(dbp[...]), axis=0, keepdims=True)
-    zero = jnp.zeros_like(db)
-    db0, db1 = jnp.where(c == 0, db, zero), jnp.where(c == 0, zero, db)
-    vown[0:1, :] = db0[:, 0:WIDTH]
-    vown[1:2, :] = db0[:, WIDTH:]
-    vown[2:3, :] = db1[:, 0:WIDTH]
-    vown[3:4, :] = db1[:, WIDTH:]
+    lane = lax.broadcasted_iota(jnp.int32, (CHUNK, 128), 1)
+    db = jnp.zeros((CHUNK, 128), F32)
+    for yy in range(NY):
+        for xx in range(NX):
+            k = yy * NX + xx
+            total = jnp.sum(dbp[k * CHUNK : (k + 1) * CHUNK, :], axis=1, keepdims=True)
+            db = jnp.where(lane == group_of(xx, yy, c), total, db)
+    for p in range(4):
+        line = dot_exact(db, hot[p][:CHUNK], ((0,), (0,)))
+        vown[p : p + 1, :] = jnp.sum(jnp.where(in_group, line, 0.0), axis=0, keepdims=True)
     vown[4:5, :] = jnp.sum(dn * xh, axis=0, keepdims=True)
     vown[5:6, :] = jnp.sum(dn, axis=0, keepdims=True)
     vown[6:7, :] = jnp.sum(cot, axis=0, keepdims=True)
@@ -240,28 +321,34 @@
     vy[y] = vown[...] + vcore[...]
     vyc = [send(vy.at[y], vy.at[y], vs.at[d], vr.at[d], to_y[d]) for d in (1, 3, 2)]
 
+    g2 = []
+
     def add_in():
         for copy in g1i:
             copy.wait_recv()
-        for q in range(NX):
+        for d in (1, 3, 2, 0):
+            q = xp[d]
             total = gin[y, q].astype(F32)
-            for d in range(3):
-                total = total + r1in[d, q].astype(F32)
+            for e in range(3):
+                total = total + r1in[e, q].astype(F32)
             s1in[q] = total.astype(BF)
-
-    def add_out():
-        for copy in g1o:
+            if d:
+                g2.append(send(s1in.at[q], r2in.at[d - 1], g2s.at[0, d - 1], g2r.at[0, d - 1], to_x[d]))
+
+    def add_out(d):
+        for copy in g1o[d]:
             copy.wait_recv()
-        for q in range(NY):
-            total = gout[q, x].astype(F32)
-            for d in range(3):
-                total = total + r1out[d, q].astype(F32)
-            s1out[q] = total.astype(BF)
-
+        q = yp[d]
+        total = gout[q, x].astype(F32)
+        for e in range(3):
+            total = total + r1out[e, q].astype(F32)
+        s1out[q] = total.astype(BF)
+        if d:
+            g2.append(send(s1out.at[q], r2out.at[d - 1], g2s.at[1, d - 1], g2r.at[1, d - 1], to_y[d]))
+
+    for d in (0, 1, 3, 2):
+        add_out(d)
     add_in()
-    g2 = [send(s1in.at[xp[d]], r2in.at[d - 1], g2s.at[0, d - 1], g2r.at[0, d - 1], to_x[d]) for d in (1, 3, 2)]
-    add_out()
-    g2 += [send(s1out.at[yp[d]], r2out.at[d - 1], g2s.at[1, d - 1], g2r.at[1, d - 1], to_y[d]) for d in (1, 3, 2)]
     for copy in vyc:
         copy.wait_recv()
     vx[x] = (vy[0] + vy[1]) + (vy[2] + vy[3])
@@ -292,12 +379,7 @@
     for d in range(NZ - 1):
         grad = grad + r3[d].astype(F32)
     grad = grad * (1.0 / math.sqrt(TOKENS))
-    omin_ref[...], ovin_ref[...], oqin_ref[...] = adamw(
-        min_ref[...], vin_ref[...], qin_ref[...], grad[0:OWN]
-    )
-    omout_ref[...], ovout_ref[...], oqout_ref[...] = adamw(
-        mout_ref[...], vout_ref[...], qout_ref[...], grad[16 : 16 + OWN]
-    )
+    grad_ref[...] = grad
     for copy in vzc:
         copy.wait_recv()
     total = vz[0]
@@ -308,25 +390,45 @@
         copy.wait_send()
 
 
+def update_kernel(
+    layer_ref, dtok_ref, vec_ref, grad_ref,
+    min_ref, vin_ref, qin_ref, mout_ref, vout_ref, qout_ref,
+    olayer_ref, odtok_ref, ogain_ref, oshift_ref, obin_ref, obout_ref,
+    omin_ref, ovin_ref, oqin_ref, omout_ref, ovout_ref, oqout_ref,
+):
+    olayer_ref[...] = layer_ref[...]
+    odtok_ref[...] = dtok_ref[...]
+    omin_ref[...], ovin_ref[...], oqin_ref[...] = adamw(
+        min_ref[...], vin_ref[...], qin_ref[...], grad_ref[0:OWN, :]
+    )
+    omout_ref[...], ovout_ref[...], oqout_ref[...] = adamw(
+        mout_ref[...], vout_ref[...], qout_ref[...], grad_ref[16 : 16 + OWN, :]
+    )
+    for p in range(4):
+        obin_ref[pl.ds(p * WIDTH, WIDTH)] = vec_ref[p : p + 1, :].reshape(WIDTH)
+    ogain_ref[...] = vec_ref[4:5, :].reshape(WIDTH)
+    oshift_ref[...] = vec_ref[5:6, :].reshape(WIDTH)
+    obout_ref[...] = vec_ref[6:7, :].reshape(WIDTH)
+
+
 def body(
     tokens, cotangent, codes_in, scales_in, codes_out, scales_out,
     layer_norm_gain, layer_norm_bias, bias_in, bias_out,
     master_in, moment_in, second_in, master_out, moment_out, second_out,
 ):
-    bias = bias_in.reshape(NZ, 2, NY, 2, NC, OWN).transpose(4, 2, 1, 3, 0, 5).reshape(NC, HIDDEN)
     vmem = pl.BlockSpec(memory_space=pltpu.VMEM)
     owned = jax.ShapeDtypeStruct((OWN, WIDTH), F32)
     dma = pltpu.SemaphoreType.DMA
-    outs = pl.pallas_call(
+    layer, d_tokens, vec, grad = pl.pallas_call(
         kernel,
         out_shape=[
             jax.ShapeDtypeStruct(tokens.shape, BF),
             jax.ShapeDtypeStruct(tokens.shape, BF),
             jax.ShapeDtypeStruct((8, WIDTH), F32),
-        ]
-        + [owned] * 6,
-        in_specs=[vmem] * 16,
-        out_specs=[vmem] * 9,
+            jax.ShapeDtypeStruct((SHARD, WIDTH), F32),
+        ],
+        in_specs=[vmem] * 10,
+        out_specs=[vmem] * 4,
         scratch_shapes=[
             pltpu.VMEM((2 * ROWS, WIDTH), BF),
             pltpu.VMEM((2 * ROWS, WIDTH), BF),
@@ -337,7 +439,7 @@
             pltpu.VMEM((NZ, SHARD, WIDTH), BF),
             pltpu.VMEM((NY, NX, CHUNK, WIDTH), BF),
             pltpu.VMEM((NY, NX, CHUNK, WIDTH), BF),
-            pltpu.VMEM((HIDDEN, 128), F32),
+            pltpu.VMEM((HIDDEN, 1), F32),
             pltpu.VMEM((HIDDEN, 128), F32),
             pltpu.VMEM((HIDDEN, 2 * ROWS), BF),
             pltpu.VMEM((HIDDEN, 2 * ROWS), BF),
@@ -360,8 +462,7 @@
             pltpu.VMEM((NZ, 8, WIDTH), F32),
             dma((2,)), dma((2,)),
             dma((7,)), dma((7,)),
-            dma((2, 3)), dma((2, 3)),
-            dma((2, 4, 3)), dma((2, 4, 3)),
+            dma((10, 4)), dma((10, 4)),
             dma((3,)), dma((3,)),
             dma((4, 3)), dma((4, 3)),
             dma((2, 3)), dma((2, 3)),
@@ -374,15 +475,22 @@
         ),
     )(
         tokens, cotangent, codes_in, scales_in, codes_out, scales_out,
-        layer_norm_gain.reshape(1, WIDTH), layer_norm_bias.reshape(1, WIDTH),
-        bias, bias_out.reshape(1, WIDTH),
-        master_in, moment_in, second_in, master_out, moment_out, second_out,
-    )
-    layer, d_tokens, vec = outs[:3]
-    d_bias_in = (
-        vec[0:4].reshape(NC, NY, 2, 2, NZ, OWN).transpose(4, 2, 1, 3, 0, 5).reshape(NC * HIDDEN)
-    )
-    return (layer, d_tokens, vec[4], vec[5], d_bias_in, vec[6]) + tuple(outs[3:])
+        layer_norm_gain, layer_norm_bias, bias_in, bias_out,
+    )
+    return tuple(
+        pl.pallas_call(
+            update_kernel,
+            out_shape=[jax.ShapeDtypeStruct(tokens.shape, BF)] * 2
+            + [jax.ShapeDtypeStruct((n,), F32) for n in (WIDTH, WIDTH, NC * HIDDEN, WIDTH)]
+            + [owned] * 6,
+            in_specs=[vmem] * 10,
+            out_specs=[vmem] * 12,
+            compiler_params=pltpu.CompilerParams(vmem_limit_bytes=32 * 2**20),
+        )(
+            layer, d_tokens, vec, grad,
+            master_in, moment_in, second_in, master_out, moment_out, second_out,
+        )
+    )
 
 
 def solution(mesh):

time: 101 us -> 85.9 us (0.85)
  local copies, waits for them, and re-layouts: 14 us -> 3.68 us
  Pallas kernels: 86 us -> 81.1 us
    pallas_call x1, Pallas kernels: 86 us -> 79.9 us  [body(): pl.pallas_call(kernel, out_shape=[jax.ShapeDtypeStruct(tokens.shape, BF),...]
    reshape x8 -> x0, local copies, waits for them, and re-layouts: 5.13 us -> none  [the longest x1 1.27 us: body(): layer_norm_gain.reshape(1, WIDTH)]
    unnamed x28 -> x20, local copies, waits for them, and re-layouts: 6.57 us -> 3.68 us
    slice x2 -> x0, local copies, waits for them, and re-layouts: 2.19 us -> none  [the longest x1 1.46 us: body(): vec[6]]
    pallas_call x0 -> x1, Pallas kernels: none -> 1.14 us  [body(): pl.pallas_call(update_kernel, out_shape=[jax.ShapeDtypeStruct(tokens.shap...]
where the time goes in v2:
time: 85.9 us; the launch traced here: 85.6 us
  Pallas kernels  81.1 us (94%)
  local copies, waits for them, and re-layouts  3.68 us (4%)
  between operations  0.87 us (1%)
    pallas_call x1, Pallas kernels, body(): pl.pallas_call(kernel, out_shape=[jax.ShapeDtypeStruct(tokens.shape, BF),...  79.9 us
    unnamed x20, local copies, waits for them, and re-layouts  3.68 us

profile of v2, /device:TPU:8, one launch (start us, length us, event | category | flops | bytes accessed | tf_op | source)
XLA Modules:
  0.0 85.6 jit_solution(16388030235464011941)
XLA Ops:
  0.7 0.0 copy-start.8
  0.7 0.0 copy-start.7
  0.7 0.0 copy-start.6
  0.7 0.0 copy-start.5
  0.7 0.0 copy-start.4
  0.7 0.0 copy-start.3
  0.7 79.9 %shard_map.247 = (bf16[1,375,640]{2,1,0:T(8,128)(2,1)}, bf16[1,375,640]{2,1,0:T(8,128)(2,1)}, f32[8,640]{1,0:T(8,128)}, f32[32,640]{1,0:T(8,128)}) custom-call(bf16[1,375,640]{2,1,0:T(8,128)(2,1)} %tok_ref.1, bf16[1,375,640]{2,1,0:T(8,128)(2,1)} %cot_ref.1, s32[10,640]{1,0:T(8,128)} %cin_ref.1, s32[10,20]{1,0:T(8,128)} %sin_ref.1, s32[10,640]{1,0:T(8,128)} %cout_ref.1, ...), custom_call_target="tpu_custom_call" | custom-call | tf_op jit(solution)/shard_map/pallas_call | solution.py:422
  80.6 0.0 copy-done.8
  80.6 0.0 copy-done.7
  80.7 0.0 copy-done.6
  80.7 0.0 copy-done.5
  80.7 0.0 copy-done.4
  80.7 0.0 copy-done.3
  80.7 0.0 copy-start
  80.7 1.0 %copy-done = bf16[1,375,640]{2,1,0:T(8,128)(2,1)S(1)} copy-done((bf16[1,375,640]{2,1,0:T(8,128)(2,1)S(1)}, bf16[1,375,640]{2,1,0:T(8,128)(2,1)}, u32[]{:S(2)}) %copy-start) | copy-done | bytes 480024
  81.7 0.0 copy-start.1
  81.7 1.0 %copy-done.1 = bf16[1,375,640]{2,1,0:T(8,128)(2,1)S(1)} copy-done((bf16[1,375,640]{2,1,0:T(8,128)(2,1)S(1)}, bf16[1,375,640]{2,1,0:T(8,128)(2,1)}, u32[]{:S(2)}) %copy-start.1) | copy-done | bytes 480024
  82.8 0.0 copy-start.2
  82.8 0.9 %copy-done.2 = f32[32,640]{1,0:T(8,128)S(1)} copy-done((f32[32,640]{1,0:T(8,128)S(1)}, f32[32,640]{1,0:T(8,128)}, u32[]{:S(2)}) %copy-start.2) | copy-done | bytes 81944
  83.6 0.0 copy-start.9
  83.6 0.7 copy-done.9
  84.4 1.1 %shard_map.248 = (bf16[1,375,640]{2,1,0:T(8,128)(2,1)}, bf16[1,375,640]{2,1,0:T(8,128)(2,1)}, f32[640]{0:T(1024)}, f32[640]{0:T(1024)}, f32[2560]{0:T(1024)}, /*...) custom-call(bf16[1,375,640]{2,1,0:T(8,128)(2,1)S(1)} %copy-done, ...), custom_call_target="tpu_custom_call" | custom-call | tf_op jit(solution)/shard_map/pallas_call | solution.py:481
Async XLA Ops:
  0.7 80.0 %copy-start.8 = (f32[10,640]{1,0:T(8,128)S(1)}, f32[10,640]{1,0:T(8,128)}, u32[]{:S(2)}) copy-start(f32[10,640]{1,0:T(8,128)} %qout_ref.1) | copy-start | bytes 76804
  0.7 80.0 %copy-start.7 = (f32[10,640]{1,0:T(8,128)S(1)}, f32[10,640]{1,0:T(8,128)}, u32[]{:S(2)}) copy-start(f32[10,640]{1,0:T(8,128)} %vout_ref.1) | copy-start | bytes 76804
  0.7 80.0 %copy-start.6 = (f32[10,640]{1,0:T(8,128)S(1)}, f32[10,640]{1,0:T(8,128)}, u32[]{:S(2)}) copy-start(f32[10,640]{1,0:T(8,128)} %mout_ref.1) | copy-start | bytes 76804
  0.7 80.0 %copy-start.5 = (f32[10,640]{1,0:T(8,128)S(1)}, f32[10,640]{1,0:T(8,128)}, u32[]{:S(2)}) copy-start(f32[10,640]{1,0:T(8,128)} %qin_ref.1) | copy-start | bytes 76804
  0.7 80.0 %copy-start.4 = (f32[10,640]{1,0:T(8,128)S(1)}, f32[10,640]{1,0:T(8,128)}, u32[]{:S(2)}) copy-start(f32[10,640]{1,0:T(8,128)} %vin_ref.1) | copy-start | bytes 76804
  0.7 80.0 %copy-start.3 = (f32[10,640]{1,0:T(8,128)S(1)}, f32[10,640]{1,0:T(8,128)}, u32[]{:S(2)}) copy-start(f32[10,640]{1,0:T(8,128)} %min_ref.1) | copy-start | bytes 76804
  80.7 1.0 %copy-start = (bf16[1,375,640]{2,1,0:T(8,128)(2,1)S(1)}, bf16[1,375,640]{2,1,0:T(8,128)(2,1)}, u32[]{:S(2)}) copy-start(bf16[1,375,640]{2,1,0:T(8,128)(2,1)} %get-tuple-element.16.layer_ref) | copy-start | bytes 1440004
  81.7 1.0 %copy-start.1 = (bf16[1,375,640]{2,1,0:T(8,128)(2,1)S(1)}, bf16[1,375,640]{2,1,0:T(8,128)(2,1)}, u32[]{:S(2)}) copy-start(bf16[1,375,640]{2,1,0:T(8,128)(2,1)} %get-tuple-element.17.dtok_ref) | copy-start | bytes 1440004
  82.8 0.9 %copy-start.2 = (f32[32,640]{1,0:T(8,128)S(1)}, f32[32,640]{1,0:T(8,128)}, u32[]{:S(2)}) copy-start(f32[32,640]{1,0:T(8,128)} %get-tuple-element.19.grad_ref) | copy-start | bytes 245764
  83.6 0.7 copy-start.9

commit v3 on v2

--- a/solution.py
+++ b/solution.py
@@ -15,6 +15,7 @@
 CHUNK = NZ * OWN
 BLOCK = NX * CHUNK
 HIDDEN = NY * BLOCK
+PACK = 112
 SHARD = 32
 TOKENS = 96000
 BF, F32 = jnp.bfloat16, jnp.float32
@@ -59,15 +60,28 @@
     return jnp.where(negative, -value, value)
 
 
-def shard_select():
-    r = lax.broadcasted_iota(jnp.int32, (2 * CHUNK, NZ * SHARD), 0)
-    col = lax.broadcasted_iota(jnp.int32, (2 * CHUNK, NZ * SHARD), 1)
+def shard_pack(shard_ref):
+    r = lax.broadcasted_iota(jnp.int32, (PACK, SHARD), 0)
+    col = lax.broadcasted_iota(jnp.int32, (PACK, SHARD), 1)
+    col = jnp.where(col < 16, jnp.where(col < OWN, col, -PACK), jnp.where(col < 16 + OWN, col - 6, -PACK))
+    out = jnp.zeros((PACK, 128), F32)
+    for j in range(5):
+        hot = (r - 2 * OWN * j == col).astype(F32).astype(BF)
+        out = out + dot_nn(hot, shard_ref[:, 128 * j : 128 * j + 128])
+    return out.astype(BF)
+
+
+def fill_select(sel_ref):
+    r = lax.broadcasted_iota(jnp.int32, (2 * CHUNK, NZ * PACK), 0)
+    col = lax.broadcasted_iota(jnp.int32, (2 * CHUNK, NZ * PACK), 1)
     second = (r >= CHUNK).astype(jnp.int32)
     r = r - CHUNK * second
     z = jnp.zeros_like(r)
     for j in range(1, NZ):
         z = z + (r >= OWN * j).astype(jnp.int32)
-    return (col == z * (SHARD - OWN) + r + 16 * second).astype(F32).astype(BF)
+    gap = col - (z * (PACK - OWN) + r + OWN * second)
+    for j in range(5):
+        sel_ref[j] = (gap == 2 * OWN * j).astype(F32).astype(BF)
 
 
 def order_mask():
@@ -98,11 +112,11 @@
 def kernel(
     tok_ref, cot_ref, cin_ref, sin_ref, cout_ref, sout_ref,
     gain_ref, shift_ref, bin_ref, bout_ref,
-    layer_ref, dtok_ref, vec_ref, grad_ref,
-    tokb, cotb, normed, xhat, rstd, shard, zbuf, win, wout, bcol, dbp, act, dpre,
+    layer_ref, dtok_ref, ogain_ref, oshift_ref, obin_ref, obout_ref, gradin_ref, gradout_ref,
+    tokv, cotv, layv, dtv, sel, tokb, cotb, normed, xhat, rstd, shard, zpk, zbuf, win, wout, bcol, dbp, act, dpre,
     gin, gout, r1in, r1out, s1in, s1out, r2in, r2out, zsend, r3,
     part, partr, vown, vcore, vy, vx, vz,
-    cs, cr, zs, zr, ws, wr, g1is, g1ir, g1os, g1or, g2s, g2r, g3s, g3r, ps, pr, vs, vr,
+    cs, cr, zs, zr, ws, wr, g1is, g1ir, g1os, g1or, g2s, g2r, g3s, g3r, ps, pr, vs, vr, ls,
 ):
     x, y, z, c = coordinates()
     xp = [lax.rem(x + d, NX) for d in range(NX)]
@@ -127,19 +141,27 @@
     for q in to_x[1:] + to_y[1:] + to_z[1:] + [to_c]:
         pl.semaphore_signal(barrier, inc=1, device_id=q, device_id_type=MESH)
 
+    loads = [
+        pltpu.make_async_copy(tok_ref, tokv, ls.at[0]),
+        pltpu.make_async_copy(cot_ref, cotv, ls.at[1]),
+    ]
+    for copy in loads:
+        copy.start()
     shard[...] = jnp.zeros_like(shard)
     shard[0:OWN, :] = decode(cin_ref[...], sin_ref[...]).astype(BF)
     shard[16 : 16 + OWN, :] = decode(cout_ref[...], sout_ref[...]).astype(BF)
-    zbuf[z] = shard[...]
-    for buf, ref in ((tokb, tok_ref), (cotb, cot_ref)):
+    zpk[...] = shard_pack(shard)
+    zbuf[z] = zpk[...]
+    pl.semaphore_wait(barrier, NX + NY + NZ - 2)
+
+    zc = [
+        send(zpk, zbuf.at[z], zs.at[d - 1], zr.at[d - 1], to_z[d])
+        for d in (4, 3, 5, 2, 6, 1, 7)
+    ]
+    for copy, buf, ref in zip(loads, (tokb, cotb), (tokv, cotv)):
+        copy.wait()
         buf[ROWS - 16 : ROWS, :] = jnp.zeros((16, WIDTH), BF)
         buf[0:FRAMES, :] = ref[0]
-    pl.semaphore_wait(barrier, NX + NY + NZ - 2)
-
-    zc = [
-        send(shard, zbuf.at[z], zs.at[d - 1], zr.at[d - 1], to_z[d])
-        for d in (4, 3, 5, 2, 6, 1, 7)
-    ]
     own, other = slice(0, ROWS), slice(ROWS, 2 * ROWS)
     cc = [
         send(buf.at[own], buf.at[other], cs.at[i], cr.at[i], to_c)
@@ -173,16 +195,18 @@
             bcol[(yy * NX + xx) * CHUNK : (yy * NX + xx + 1) * CHUNK, :] = jnp.where(
                 c == 0, bias[:CHUNK, g : g + 1], bias[:CHUNK, g + 1 : g + 2]
             )
-    select = shard_select()
+    fill_select(sel)
     for copy in cc:
         copy.wait_recv()
     norm(other)
 
     for copy in zc:
         copy.wait_recv()
-    w = dot_nn(select, zbuf[...].reshape(NZ * SHARD, WIDTH)).astype(BF)
-    win[y, x] = w[:CHUNK]
-    wout[y, x] = w[CHUNK:]
+    lines = zbuf[...].reshape(NZ * PACK, 128)
+    for j in range(5):
+        w = dot_nn(sel[j], lines).astype(BF)
+        win[y, x, :, 128 * j : 128 * j + 128] = w[:CHUNK]
+        wout[y, x, :, 128 * j : 128 * j + 128] = w[CHUNK:]
 
     to = ((to_x[1], to_x[3]), (to_y[1], to_y[3]))
 
@@ -292,7 +316,12 @@
     cot = cotb[own, :].astype(F32)
     pc[0].wait_recv()
     layer = tokb[own, :].astype(F32) + (part[0, 0] + partr[0]) + bout_ref[...].reshape(1, WIDTH)
-    layer_ref[0] = layer.astype(BF)[0:FRAMES]
+    layv[0] = layer.astype(BF)[0:FRAMES]
+    stores = [
+        pltpu.make_async_copy(layv, layer_ref, ls.at[2]),
+        pltpu.make_async_copy(dtv, dtok_ref, ls.at[3]),
+    ]
+    stores[0].start()
     pc[1].wait_recv()
     dn = part[1, 0] + partr[1]
     xh = xhat[...]
@@ -300,7 +329,8 @@
     dt = cot + rstd[...] * (
         dx - jnp.mean(dx, axis=-1, keepdims=True) - xh * jnp.mean(dx * xh, axis=-1, keepdims=True)
     )
-    dtok_ref[0] = dt.astype(BF)[0:FRAMES]
+    dtv[0] = dt.astype(BF)[0:FRAMES]
+    stores[1].start()
 
     lane = lax.broadcasted_iota(jnp.int32, (CHUNK, 128), 1)
     db = jnp.zeros((CHUNK, 128), F32)
@@ -318,8 +348,8 @@
     vown[7:8, :] = jnp.zeros((1, WIDTH), F32)
     vc = send(vown, vcore, vs.at[0], vr.at[0], to_c)
     vc.wait_recv()
-    vy[y] = vown[...] + vcore[...]
-    vyc = [send(vy.at[y], vy.at[y], vs.at[d], vr.at[d], to_y[d]) for d in (1, 3, 2)]
+    vz[z] = vown[...] + vcore[...]
+    vzc = [send(vz.at[z], vz.at[z], vs.at[6 + d], vr.at[6 + d], to_z[d]) for d in (4, 3, 5, 2, 6, 1, 7)]
 
     g2 = []
 
@@ -346,9 +376,17 @@
         if d:
             g2.append(send(s1out.at[q], r2out.at[d - 1], g2s.at[1, d - 1], g2r.at[1, d - 1], to_y[d]))
 
-    for d in (0, 1, 3, 2):
+    for d in (0, 1, 3):
         add_out(d)
+    for copy in vzc:
+        copy.wait_recv()
+    total = vz[0]
+    for q in range(1, NZ):
+        total = total + vz[q]
+    vy[y] = total
+    vyc = [send(vy.at[y], vy.at[y], vs.at[d], vr.at[d], to_y[d]) for d in (1, 3, 2)]
     add_in()
+    add_out(2)
     for copy in vyc:
         copy.wait_recv()
     vx[x] = (vy[0] + vy[1]) + (vy[2] + vy[3])
@@ -363,52 +401,37 @@
             total = total + got[d].astype(F32)
         sums.append(total.astype(BF))
     both = jnp.concatenate(sums, axis=0)
-    zsend[...] = dot_tn(select, both).astype(BF).reshape(NZ, SHARD, WIDTH)
+    packed = jnp.zeros((NZ * PACK, 128), F32)
+    for j in range(5):
+        packed = packed + dot_tn(sel[j], both[:, 128 * j : 128 * j + 128])
+    zsend[...] = packed.astype(BF).reshape(NZ, PACK, 128)
     g3 = [
         send(zsend.at[zp[d]], r3.at[d - 1], g3s.at[d - 1], g3r.at[d - 1], to_z[d])
         for d in (4, 3, 5, 2, 6, 1, 7)
     ]
+
     for copy in vxc:
         copy.wait_recv()
-    vz[z] = (vx[0] + vx[1]) + (vx[2] + vx[3])
-    vzc = [send(vz.at[z], vz.at[z], vs.at[6 + d], vr.at[6 + d], to_z[d]) for d in (4, 3, 5, 2, 6, 1, 7)]
+    total = (vx[0] + vx[1]) + (vx[2] + vx[3])
+    for p in range(4):
+        obin_ref[pl.ds(p * WIDTH, WIDTH)] = total[p : p + 1].reshape(WIDTH)
+    ogain_ref[...] = total[4:5].reshape(WIDTH)
+    oshift_ref[...] = total[5:6].reshape(WIDTH)
+    obout_ref[...] = total[6:7].reshape(WIDTH)
 
     for copy in g3:
         copy.wait_recv()
     grad = zsend[z].astype(F32)
     for d in range(NZ - 1):
         grad = grad + r3[d].astype(F32)
-    grad = grad * (1.0 / math.sqrt(TOKENS))
-    grad_ref[...] = grad
-    for copy in vzc:
-        copy.wait_recv()
-    total = vz[0]
-    for q in range(1, NZ):
-        total = total + vz[q]
-    vec_ref[...] = total * (1.0 / math.sqrt(TOKENS))
+    for j in range(5):
+        cols = slice(128 * j, 128 * j + 128)
+        gradin_ref[:, cols] = grad[2 * OWN * j : 2 * OWN * j + OWN]
+        gradout_ref[:, cols] = grad[2 * OWN * j + OWN : 2 * OWN * (j + 1)]
+    for copy in stores:
+        copy.wait()
     for copy in pending:
         copy.wait_send()
-
-
-def update_kernel(
-    layer_ref, dtok_ref, vec_ref, grad_ref,
-    min_ref, vin_ref, qin_ref, mout_ref, vout_ref, qout_ref,
-    olayer_ref, odtok_ref, ogain_ref, oshift_ref, obin_ref, obout_ref,
-    omin_ref, ovin_ref, oqin_ref, omout_ref, ovout_ref, oqout_ref,
-):
-    olayer_ref[...] = layer_ref[...]
-    odtok_ref[...] = dtok_ref[...]
-    omin_ref[...], ovin_ref[...], oqin_ref[...] = adamw(
-        min_ref[...], vin_ref[...], qin_ref[...], grad_ref[0:OWN, :]
-    )
-    omout_ref[...], ovout_ref[...], oqout_ref[...] = adamw(
-        mout_ref[...], vout_ref[...], qout_ref[...], grad_ref[16 : 16 + OWN, :]
-    )
-    for p in range(4):
-        obin_ref[pl.ds(p * WIDTH, WIDTH)] = vec_ref[p : p + 1, :].reshape(WIDTH)
-    ogain_ref[...] = vec_ref[4:5, :].reshape(WIDTH)
-    oshift_ref[...] = vec_ref[5:6, :].reshape(WIDTH)
-    obout_ref[...] = vec_ref[6:7, :].reshape(WIDTH)
 
 
 def body(
@@ -419,24 +442,26 @@
     vmem = pl.BlockSpec(memory_space=pltpu.VMEM)
     owned = jax.ShapeDtypeStruct((OWN, WIDTH), F32)
     dma = pltpu.SemaphoreType.DMA
-    layer, d_tokens, vec, grad = pl.pallas_call(
+    hbm = pl.BlockSpec(memory_space=pl.ANY)
+    rounded = pltpu.VMEM(tokens.shape, BF)
+    outs = pl.pallas_call(
         kernel,
-        out_shape=[
-            jax.ShapeDtypeStruct(tokens.shape, BF),
-            jax.ShapeDtypeStruct(tokens.shape, BF),
-            jax.ShapeDtypeStruct((8, WIDTH), F32),
-            jax.ShapeDtypeStruct((SHARD, WIDTH), F32),
-        ],
-        in_specs=[vmem] * 10,
-        out_specs=[vmem] * 4,
-        scratch_shapes=[
+        out_shape=[jax.ShapeDtypeStruct(tokens.shape, BF)] * 2
+        + [jax.ShapeDtypeStruct((n,), F32) for n in (WIDTH, WIDTH, NC * HIDDEN, WIDTH)]
+        + [owned] * 2,
+        in_specs=[hbm] * 2 + [vmem] * 8,
+        out_specs=[hbm] * 2 + [vmem] * 6,
+        scratch_shapes=[rounded] * 4
+        + [
+            pltpu.VMEM((5, 2 * CHUNK, NZ * PACK), BF),
             pltpu.VMEM((2 * ROWS, WIDTH), BF),
             pltpu.VMEM((2 * ROWS, WIDTH), BF),
             pltpu.VMEM((2 * ROWS, WIDTH), BF),
             pltpu.VMEM((ROWS, WIDTH), F32),
             pltpu.VMEM((ROWS, 1), F32),
             pltpu.VMEM((SHARD, WIDTH), BF),
-            pltpu.VMEM((NZ, SHARD, WIDTH), BF),
+            pltpu.VMEM((PACK, 128), BF),
+            pltpu.VMEM((NZ, PACK, 128), BF),
             pltpu.VMEM((NY, NX, CHUNK, WIDTH), BF),
             pltpu.VMEM((NY, NX, CHUNK, WIDTH), BF),
             pltpu.VMEM((HIDDEN, 1), F32),
@@ -451,8 +476,8 @@
             pltpu.VMEM((NY, CHUNK, WIDTH), BF),
             pltpu.VMEM((NX - 1, CHUNK, WIDTH), BF),
             pltpu.VMEM((NY - 1, CHUNK, WIDTH), BF),
-            pltpu.VMEM((NZ, SHARD, WIDTH), BF),
-            pltpu.VMEM((NZ - 1, SHARD, WIDTH), BF),
+            pltpu.VMEM((NZ, PACK, 128), BF),
+            pltpu.VMEM((NZ - 1, PACK, 128), BF),
             pltpu.VMEM((2, 2, ROWS, WIDTH), F32),
             pltpu.VMEM((2, ROWS, WIDTH), F32),
             pltpu.VMEM((8, WIDTH), F32),
@@ -469,6 +494,7 @@
             dma((7,)), dma((7,)),
             dma((2,)), dma((2,)),
             dma((14,)), dma((14,)),
+            dma((4,)),
         ],
         compiler_params=pltpu.CompilerParams(
             collective_id=0, has_side_effects=True, vmem_limit_bytes=56 * 2**20
@@ -477,19 +503,12 @@
         tokens, cotangent, codes_in, scales_in, codes_out, scales_out,
         layer_norm_gain, layer_norm_bias, bias_in, bias_out,
     )
-    return tuple(
-        pl.pallas_call(
-            update_kernel,
-            out_shape=[jax.ShapeDtypeStruct(tokens.shape, BF)] * 2
-            + [jax.ShapeDtypeStruct((n,), F32) for n in (WIDTH, WIDTH, NC * HIDDEN, WIDTH)]
-            + [owned] * 6,
-            in_specs=[vmem] * 10,
-            out_specs=[vmem] * 12,
-            compiler_params=pltpu.CompilerParams(vmem_limit_bytes=32 * 2**20),
-        )(
-            layer, d_tokens, vec, grad,
-            master_in, moment_in, second_in, master_out, moment_out, second_out,
-        )
+    sums = [total * (1.0 / math.sqrt(TOKENS)) for total in outs[2:]]
+    return (
+        tuple(outs[:2])
+        + tuple(sums[:4])
+        + adamw(master_in, moment_in, second_in, sums[4])
+        + adamw(master_out, moment_out, second_out, sums[5])
     )
 
 

time: 85.9 us -> 81.9 us (0.953)
  Pallas kernels: 81.1 us -> 73.3 us
  other arithmetic: 0 us -> 5.43 us
  local copies, waits for them, and re-layouts: 3.68 us -> 2 us
    pallas_call x2 -> x1, Pallas kernels: 81.1 us -> 73.3 us  [body(): pl.pallas_call(kernel, out_shape=[jax.ShapeDtypeStruct(tokens.shape, BF)]...]
    mul x0 -> x3, other arithmetic: none -> 3.92 us  [body(): sums = [total * (1.0 / math.sqrt(TOKENS)) for total in outs[2:]]]
    unnamed x20 -> x18, local copies, waits for them, and re-layouts: 3.68 us -> 2 us
    sub x0 -> x1, other arithmetic: none -> 1.52 us  [adamw(): master - 0.001 * (new_moment / (jnp.sqrt(new_second) + 1e-08) + 0.1 * mas...]
where the time goes in v3:
time: 81.9 us; the launch traced here: 81.5 us
  Pallas kernels  73.3 us (89%)
  other arithmetic  5.43 us (7%)
  local copies, waits for them, and re-layouts  2 us (2%)
    pallas_call x1, Pallas kernels, body(): pl.pallas_call(kernel, out_shape=[jax.ShapeDtypeStruct(tokens.shape, BF)]...  73.3 us
    mul x3, other arithmetic, body(): sums = [total * (1.0 / math.sqrt(TOKENS)) for total in outs[2:]]  3.92 us
    unnamed x18, local copies, waits for them, and re-layouts  2 us

profile of v3, /device:TPU:8, one launch (start us, length us, event | category | flops | bytes accessed | tf_op | source)
XLA Modules:
  0.0 81.5 jit_solution(4226574818872668366)
XLA Ops:
  0.7 0.0 copy-start.2
  0.7 0.0 copy-start.3
  0.7 0.0 copy-start.4
  0.7 0.0 copy-start.5
  0.7 0.0 copy-start.6
  0.7 0.0 copy-start.7
  0.7 73.3 %shard_map.247 = (bf16[1,375,640]{2,1,0:T(8,128)(2,1)}, bf16[1,375,640]{2,1,0:T(8,128)(2,1)}, f32[640]{0:T(1024)}, f32[640]{0:T(1024)}, f32[2560]{0:T(1024)}, /*...) custom-call(bf16[1,375,640]{2,1,0:T(8,128)(2,1)} %tok_ref.1, bf16[1,375,640]{2,1,0:T(8,128)(2,1)} %cot_ref.1, ...), custom_call_target="tpu_custom_call" | custom-call | tf_op jit(solution)/shard_map/pallas_call | solution.py:447
  74.0 0.0 copy-start.1
  74.1 1.3 %broadcast_multiply_fusion.3 = f32[640]{0:T(1024)} fusion(f32[640]{0:T(1024)} %get-tuple-element.22), kind=kLoop, calls=%fused_computation.9 | loop fusion | flops 640 | bytes 5120 | tf_op jit(solution)/shard_map/mul | solution.py:506
  75.4 1.3 %broadcast_multiply_fusion.1 = (f32[640]{0:T(1024)}, f32[640]{0:T(1024)}) fusion(f32[640]{0:T(1024)} %get-tuple-element.25, f32[640]{0:T(1024)} %get-tuple-element.23), kind=kLoop, calls=%fused_computation.7 | loop fusion | flops 1280 | bytes 10240 | tf_op jit(solution)/shard_map/mul | solution.py:506
  76.7 1.3 %broadcast_multiply_fusion = f32[2560]{0:T(1024)} fusion(f32[2560]{0:T(1024)} %get-tuple-element.24), kind=kLoop, calls=%fused_computation.6 | loop fusion | flops 2560 | bytes 20480 | tf_op jit(solution)/shard_map/mul | solution.py:506
  78.0 0.0 copy-done.2
  78.0 0.0 copy-done.3
  78.0 0.0 copy-done.4
  78.0 0.0 copy-done.5
  78.0 0.0 copy-done.6
  78.0 0.0 copy-done.7
  78.0 1.5 %multiply_subtract_fusion = (f32[10,640]{1,0:T(8,128)}, f32[10,640]{1,0:T(8,128)}, f32[10,640]{1,0:T(8,128)}, f32[10,640]{1,0:T(8,128)}, f32[10,640]{1,0:T(8,128)}, /*index=5*/f32[10,640]{1,0:T(8,128)}) fusion(f32[10,640]{1,0:T(8,128)S(1)} %copy-done.2, f32[10,640]{1,0:T(8,128)} %get-tuple-element.27, f32[10,640]{1,0:T(8,128)S(1)} %copy-done.3, ...), kind=kLoop, calls=%fused_computation | loop fusion | flops 179200 | bytes 358400 | tf_op jit(solution)/shard_map/sub | solution.py:108
  79.5 0.0 copy-done.1
  79.5 0.0 copy-start
  79.5 0.8 copy.30
  80.3 0.4 copy-done
  80.7 0.8 copy.31
Async XLA Ops:
  0.7 77.3 %copy-start.2 = (f32[10,640]{1,0:T(8,128)S(1)}, f32[10,640]{1,0:T(8,128)}, u32[]{:S(2)}) copy-start(f32[10,640]{1,0:T(8,128)} %param.29) | copy-start | bytes 76804
  0.7 77.3 %copy-start.3 = (f32[10,640]{1,0:T(8,128)S(1)}, f32[10,640]{1,0:T(8,128)}, u32[]{:S(2)}) copy-start(f32[10,640]{1,0:T(8,128)} %param.31) | copy-start | bytes 76804
  0.7 77.3 %copy-start.4 = (f32[10,640]{1,0:T(8,128)S(1)}, f32[10,640]{1,0:T(8,128)}, u32[]{:S(2)}) copy-start(f32[10,640]{1,0:T(8,128)} %param.30) | copy-start | bytes 76804
  0.7 77.3 %copy-start.5 = (f32[10,640]{1,0:T(8,128)S(1)}, f32[10,640]{1,0:T(8,128)}, u32[]{:S(2)}) copy-start(f32[10,640]{1,0:T(8,128)} %param.26) | copy-start | bytes 76804
  0.7 77.3 %copy-start.6 = (f32[10,640]{1,0:T(8,128)S(1)}, f32[10,640]{1,0:T(8,128)}, u32[]{:S(2)}) copy-start(f32[10,640]{1,0:T(8,128)} %param.28) | copy-start | bytes 76804
  0.7 77.3 %copy-start.7 = (f32[10,640]{1,0:T(8,128)S(1)}, f32[10,640]{1,0:T(8,128)}, u32[]{:S(2)}) copy-start(f32[10,640]{1,0:T(8,128)} %param.27) | copy-start | bytes 76804
  74.0 5.5 %copy-start.1 = (bf16[1,375,640]{2,1,0:T(8,128)(2,1)S(1)}, bf16[1,375,640]{2,1,0:T(8,128)(2,1)}, u32[]{:S(2)}) copy-start(bf16[1,375,640]{2,1,0:T(8,128)(2,1)} %get-tuple-element.51) | copy-start | bytes 1440004
  79.5 1.2 %copy-start = (bf16[1,375,640]{2,1,0:T(8,128)(2,1)S(1)}, bf16[1,375,640]{2,1,0:T(8,128)(2,1)}, u32[]{:S(2)}) copy-start(bf16[1,375,640]{2,1,0:T(8,128)(2,1)} %get-tuple-element.52) | copy-start | bytes 1440004

commit v4 on v3

--- a/solution.py
+++ b/solution.py
@@ -16,6 +16,8 @@
 BLOCK = NX * CHUNK
 HIDDEN = NY * BLOCK
 PACK = 112
+PLACE = (0, 20, 40, 64, 84)
+PARTS = ((slice(0, 384), slice(0, 64), (0, 1, 2)), (slice(384, 640), slice(64, 112), (3, 4)))
 SHARD = 32
 TOKENS = 96000
 BF, F32 = jnp.bfloat16, jnp.float32
@@ -66,7 +68,7 @@
     col = jnp.where(col < 16, jnp.where(col < OWN, col, -PACK), jnp.where(col < 16 + OWN, col - 6, -PACK))
     out = jnp.zeros((PACK, 128), F32)
     for j in range(5):
-        hot = (r - 2 * OWN * j == col).astype(F32).astype(BF)
+        hot = (r - PLACE[j] == col).astype(F32).astype(BF)
         out = out + dot_nn(hot, shard_ref[:, 128 * j : 128 * j + 128])
     return out.astype(BF)
 
@@ -81,7 +83,7 @@
         z = z + (r >= OWN * j).astype(jnp.int32)
     gap = col - (z * (PACK - OWN) + r + OWN * second)
     for j in range(5):
-        sel_ref[j] = (gap == 2 * OWN * j).astype(F32).astype(BF)
+        sel_ref[j] = (gap == PLACE[j]).astype(F32).astype(BF)
 
 
 def order_mask():
@@ -259,7 +261,7 @@
             later_in[p].forward(k)
             later_out[p].forward(k)
 
-    g1i, g1o = [], {}
+    g1i, g1o = ([], []), ({}, {})
 
     def block(d):
         by = yp[d]
@@ -279,12 +281,20 @@
         gin[by] = dot_nn(dp, normed[...]).astype(BF).reshape(NX, CHUNK, WIDTH)
         gout[by] = dot_nn(a, cotb[...]).astype(BF).reshape(NX, CHUNK, WIDTH)
 
-    def block_send(d):
-        by = yp[d]
+    def block_send(d, h):
+        by, cols = yp[d], PARTS[h][0]
         if d:
-            g1i.append(send(gin.at[by], r1in.at[d - 1], g1is.at[d - 1], g1ir.at[d - 1], to_y[d]))
-        g1o[d] = [
-            send(gout.at[by, xp[e]], r1out.at[e - 1, by], g1os.at[d, e - 1], g1or.at[d, e - 1], to_x[e])
+            g1i[h].append(
+                send(
+                    gin.at[by, :, :, cols], r1in.at[d - 1, :, :, cols],
+                    g1is.at[h, d - 1], g1ir.at[h, d - 1], to_y[d],
+                )
+            )
+        g1o[h][d] = [
+            send(
+                gout.at[by, xp[e], :, cols], r1out.at[e - 1, by, :, cols],
+                g1os.at[h, d, e - 1], g1or.at[h, d, e - 1], to_x[e],
+            )
             for e in (2, 1, 3)
         ]
 
@@ -293,16 +303,19 @@
     for k in (0, 1):
         later_in[2].forward(k)
         later_out[2].forward(k)
-    block_send(0)
+    block_send(0, 0)
+    block_send(0, 1)
     for p in (1, 3):
         later_out[p].finish()
         block(p)
-        block_send(p)
+        block_send(p, 0)
     later_out[2].finish()
     for p in range(4):
         later_in[p].finish()
     block(2)
-    block_send(2)
+    block_send(2, 0)
+    for p in (1, 3, 2):
+        block_send(p, 1)
 
     wi = win[...].reshape(HIDDEN, WIDTH)
     wo = wout[...].reshape(HIDDEN, WIDTH)
@@ -351,33 +364,45 @@
     vz[z] = vown[...] + vcore[...]
     vzc = [send(vz.at[z], vz.at[z], vs.at[6 + d], vr.at[6 + d], to_z[d]) for d in (4, 3, 5, 2, 6, 1, 7)]
 
-    g2 = []
-
-    def add_in():
-        for copy in g1i:
+    g2 = ([], [])
+
+    def add_in(h):
+        cols = PARTS[h][0]
+        for copy in g1i[h]:
             copy.wait_recv()
         for d in (1, 3, 2, 0):
             q = xp[d]
-            total = gin[y, q].astype(F32)
+            total = gin[y, q, :, cols].astype(F32)
             for e in range(3):
-                total = total + r1in[e, q].astype(F32)
-            s1in[q] = total.astype(BF)
+                total = total + r1in[e, q, :, cols].astype(F32)
+            s1in[q, :, cols] = total.astype(BF)
             if d:
-                g2.append(send(s1in.at[q], r2in.at[d - 1], g2s.at[0, d - 1], g2r.at[0, d - 1], to_x[d]))
-
-    def add_out(d):
-        for copy in g1o[d]:
+                g2[h].append(
+                    send(
+                        s1in.at[q, :, cols], r2in.at[d - 1, :, cols],
+                        g2s.at[h, 0, d - 1], g2r.at[h, 0, d - 1], to_x[d],
+                    )
+                )
+
+    def add_out(d, h):
+        cols = PARTS[h][0]
+        for copy in g1o[h][d]:
             copy.wait_recv()
         q = yp[d]
-        total = gout[q, x].astype(F32)
+        total = gout[q, x, :, cols].astype(F32)
         for e in range(3):
-            total = total + r1out[e, q].astype(F32)
-        s1out[q] = total.astype(BF)
+            total = total + r1out[e, q, :, cols].astype(F32)
+        s1out[q, :, cols] = total.astype(BF)
         if d:
-            g2.append(send(s1out.at[q], r2out.at[d - 1], g2s.at[1, d - 1], g2r.at[1, d - 1], to_y[d]))
+            g2[h].append(
+                send(
+                    s1out.at[q, :, cols], r2out.at[d - 1, :, cols],
+                    g2s.at[h, 1, d - 1], g2r.at[h, 1, d - 1], to_y[d],
+                )
+            )
 
     for d in (0, 1, 3):
-        add_out(d)
+        add_out(d, 0)
     for copy in vzc:
         copy.wait_recv()
     total = vz[0]
@@ -385,34 +410,39 @@
         total = total + vz[q]
     vy[y] = total
     vyc = [send(vy.at[y], vy.at[y], vs.at[d], vr.at[d], to_y[d]) for d in (1, 3, 2)]
-    add_in()
-    add_out(2)
+    add_in(0)
+    add_out(2, 0)
+    for d in (0, 1, 3):
+        add_out(d, 1)
+    add_in(1)
+    add_out(2, 1)
     for copy in vyc:
         copy.wait_recv()
     vx[x] = (vy[0] + vy[1]) + (vy[2] + vy[3])
     vxc = [send(vx.at[x], vx.at[x], vs.at[3 + d], vr.at[3 + d], to_x[d]) for d in (1, 3, 2)]
 
-    for copy in g2:
-        copy.wait_recv()
-    sums = []
-    for first, got in ((s1in[x], r2in), (s1out[y], r2out)):
-        total = first.astype(F32)
-        for d in range(3):
-            total = total + got[d].astype(F32)
-        sums.append(total.astype(BF))
-    both = jnp.concatenate(sums, axis=0)
-    packed = jnp.zeros((NZ * PACK, 128), F32)
-    for j in range(5):
-        packed = packed + dot_tn(sel[j], both[:, 128 * j : 128 * j + 128])
-    zsend[...] = packed.astype(BF).reshape(NZ, PACK, 128)
-    g3 = [
-        send(zsend.at[zp[d]], r3.at[d - 1], g3s.at[d - 1], g3r.at[d - 1], to_z[d])
-        for d in (4, 3, 5, 2, 6, 1, 7)
-    ]
-
+    g3 = []
+    for h, (cols, rows, groups) in enumerate(PARTS):
+        for copy in g2[h]:
+            copy.wait_recv()
+        sums = []
+        for first, got in ((s1in[x, :, cols], r2in), (s1out[y, :, cols], r2out)):
+            total = first.astype(F32)
+            for d in range(3):
+                total = total + got[d, :, cols].astype(F32)
+            sums.append(total.astype(BF))
+        both = jnp.concatenate(sums, axis=0)
+        packed = jnp.zeros((NZ * PACK, 128), F32)
+        for k, j in enumerate(groups):
+            packed = packed + dot_tn(sel[j], both[:, 128 * k : 128 * k + 128])
+        zsend[:, rows, :] = packed.astype(BF).reshape(NZ, PACK, 128)[:, rows]
+        g3 += [
+            send(zsend.at[zp[d], rows], r3.at[d - 1, rows], g3s.at[h, d - 1], g3r.at[h, d - 1], to_z[d])
+            for d in (4, 3, 5, 2, 6, 1, 7)
+        ]
     for copy in vxc:
         copy.wait_recv()
-    total = (vx[0] + vx[1]) + (vx[2] + vx[3])
+    total = ((vx[0] + vx[1]) + (vx[2] + vx[3])) * (1.0 / math.sqrt(TOKENS))
     for p in range(4):
         obin_ref[pl.ds(p * WIDTH, WIDTH)] = total[p : p + 1].reshape(WIDTH)
     ogain_ref[...] = total[4:5].reshape(WIDTH)
@@ -426,8 +456,8 @@
         grad = grad + r3[d].astype(F32)
     for j in range(5):
         cols = slice(128 * j, 128 * j + 128)
-        gradin_ref[:, cols] = grad[2 * OWN * j : 2 * OWN * j + OWN]
-        gradout_ref[:, cols] = grad[2 * OWN * j + OWN : 2 * OWN * (j + 1)]
+        gradin_ref[:, cols] = grad[PLACE[j] : PLACE[j] + OWN]
+        gradout_ref[:, cols] = grad[PLACE[j] + OWN : PLACE[j] + 2 * OWN]
     for copy in stores:
         copy.wait()
     for copy in pending:
@@ -488,10 +518,10 @@
             dma((2,)), dma((2,)),
             dma((7,)), dma((7,)),
             dma((10, 4)), dma((10, 4)),
-            dma((3,)), dma((3,)),
-            dma((4, 3)), dma((4, 3)),
             dma((2, 3)), dma((2, 3)),
-            dma((7,)), dma((7,)),
+            dma((2, 4, 3)), dma((2, 4, 3)),
+            dma((2, 2, 3)), dma((2, 2, 3)),
+            dma((2, 7)), dma((2, 7)),
             dma((2,)), dma((2,)),
             dma((14,)), dma((14,)),
             dma((4,)),
@@ -503,12 +533,11 @@
         tokens, cotangent, codes_in, scales_in, codes_out, scales_out,
         layer_norm_gain, layer_norm_bias, bias_in, bias_out,
     )
-    sums = [total * (1.0 / math.sqrt(TOKENS)) for total in outs[2:]]
+    sums = [total * (1.0 / math.sqrt(TOKENS)) for total in outs[6:]]
     return (
-        tuple(outs[:2])
-        + tuple(sums[:4])
-        + adamw(master_in, moment_in, second_in, sums[4])
-        + adamw(master_out, moment_out, second_out, sums[5])
+        tuple(outs[:6])
+        + adamw(master_in, moment_in, second_in, sums[0])
+        + adamw(master_out, moment_out, second_out, sums[1])
     )
 
 

time: 81.9 us -> 79.5 us (0.971)
  other arithmetic: 5.43 us -> 1.56 us
  local copies, waits for them, and re-layouts: 2 us -> 4.48 us
  Pallas kernels: 73.3 us -> 72.4 us
    mul x3 -> x0, other arithmetic: 3.92 us -> none  [body(): sums = [total * (1.0 / math.sqrt(TOKENS)) for total in outs[2:]]]
    unnamed x18 -> x30, local copies, waits for them, and re-layouts: 2 us -> 4.48 us
    pallas_call x1, Pallas kernels: 73.3 us -> 72.4 us  [body(): pl.pallas_call(kernel, out_shape=[jax.ShapeDtypeStruct(tokens.shape, BF)]...]
where the time goes in v4:
time: 79.5 us; the launch traced here: 79.2 us
  Pallas kernels  72.4 us (91%)
  local copies, waits for them, and re-layouts  4.48 us (6%)
  other arithmetic  1.56 us (2%)
    pallas_call x1, Pallas kernels, body(): pl.pallas_call(kernel, out_shape=[jax.ShapeDtypeStruct(tokens.shape, BF)]...  72.4 us
    unnamed x30, local copies, waits for them, and re-layouts  4.48 us

profile of v4, /device:TPU:8, one launch (start us, length us, event | category | flops | bytes accessed | tf_op | source)
XLA Modules:
  0.0 79.2 jit_solution(7390673907912161137)
XLA Ops:
  0.7 0.0 copy-start.2
  0.7 0.0 copy-start.3
  0.7 0.0 copy-start.4
  0.7 0.0 copy-start.5
  0.7 0.0 copy-start.6
  0.7 0.0 copy-start.7
  0.7 72.4 %shard_map.247 = (bf16[1,375,640]{2,1,0:T(8,128)(2,1)}, bf16[1,375,640]{2,1,0:T(8,128)(2,1)}, f32[640]{0:T(1024)}, f32[640]{0:T(1024)}, f32[2560]{0:T(1024)}, /*...) custom-call(bf16[1,375,640]{2,1,0:T(8,128)(2,1)} %tok_ref.1, bf16[1,375,640]{2,1,0:T(8,128)(2,1)} %cot_ref.1, ...), custom_call_target="tpu_custom_call" | custom-call | tf_op jit(solution)/shard_map/pallas_call | solution.py:477
  73.1 0.0 copy-start.1
  73.2 0.0 copy-done.2
  73.2 0.0 copy-done.3
  73.2 0.0 copy-done.4
  73.2 0.0 copy-done.5
  73.2 0.0 copy-done.6
  73.2 0.0 copy-done.7
  73.2 1.6 %multiply_subtract_fusion = (f32[10,640]{1,0:T(8,128)}, f32[10,640]{1,0:T(8,128)}, f32[10,640]{1,0:T(8,128)}, f32[10,640]{1,0:T(8,128)}, f32[10,640]{1,0:T(8,128)}, /*index=5*/f32[10,640]{1,0:T(8,128)}) fusion(f32[10,640]{1,0:T(8,128)S(1)} %copy-done.2, f32[10,640]{1,0:T(8,128)} %get-tuple-element.27, f32[10,640]{1,0:T(8,128)S(1)} %copy-done.3, ...), kind=kLoop, calls=%fused_computation | loop fusion | flops 179200 | bytes 358400 | tf_op jit(solution)/shard_map/sub | solution.py:110
  74.8 0.0 copy-done.1
  74.8 0.0 copy-start
  74.8 0.8 copy.34
  75.5 0.4 copy-done
  76.0 0.0 copy-start.11
  76.0 0.0 copy-start.10
  76.0 0.8 copy.35
  76.8 0.0 copy-done.11
  76.8 0.0 copy-start.8
  76.8 0.6 copy.36
  77.4 0.0 copy-done.10
  77.4 0.6 copy.37
  77.9 0.0 copy-done.8
  78.0 0.0 copy-start.9
  78.0 0.6 copy.38
  78.6 0.1 copy-done.9
  78.6 0.6 copy.39
Async XLA Ops:
  0.7 72.5 %copy-start.2 = (f32[10,640]{1,0:T(8,128)S(1)}, f32[10,640]{1,0:T(8,128)}, u32[]{:S(2)}) copy-start(f32[10,640]{1,0:T(8,128)} %param.29) | copy-start | bytes 76804
  0.7 72.5 %copy-start.3 = (f32[10,640]{1,0:T(8,128)S(1)}, f32[10,640]{1,0:T(8,128)}, u32[]{:S(2)}) copy-start(f32[10,640]{1,0:T(8,128)} %param.31) | copy-start | bytes 76804
  0.7 72.5 %copy-start.4 = (f32[10,640]{1,0:T(8,128)S(1)}, f32[10,640]{1,0:T(8,128)}, u32[]{:S(2)}) copy-start(f32[10,640]{1,0:T(8,128)} %param.30) | copy-start | bytes 76804
  0.7 72.5 %copy-start.5 = (f32[10,640]{1,0:T(8,128)S(1)}, f32[10,640]{1,0:T(8,128)}, u32[]{:S(2)}) copy-start(f32[10,640]{1,0:T(8,128)} %param.26) | copy-start | bytes 76804
  0.7 72.5 %copy-start.6 = (f32[10,640]{1,0:T(8,128)S(1)}, f32[10,640]{1,0:T(8,128)}, u32[]{:S(2)}) copy-start(f32[10,640]{1,0:T(8,128)} %param.28) | copy-start | bytes 76804
  0.7 72.5 %copy-start.7 = (f32[10,640]{1,0:T(8,128)S(1)}, f32[10,640]{1,0:T(8,128)}, u32[]{:S(2)}) copy-start(f32[10,640]{1,0:T(8,128)} %param.27) | copy-start | bytes 76804
  73.1 1.6 %copy-start.1 = (bf16[1,375,640]{2,1,0:T(8,128)(2,1)S(1)}, bf16[1,375,640]{2,1,0:T(8,128)(2,1)}, u32[]{:S(2)}) copy-start(bf16[1,375,640]{2,1,0:T(8,128)(2,1)} %get-tuple-element.49) | copy-start | bytes 1440004
  74.8 1.2 %copy-start = (bf16[1,375,640]{2,1,0:T(8,128)(2,1)S(1)}, bf16[1,375,640]{2,1,0:T(8,128)(2,1)}, u32[]{:S(2)}) copy-start(bf16[1,375,640]{2,1,0:T(8,128)(2,1)} %get-tuple-element.50) | copy-start | bytes 1440004
  76.0 0.8 copy-start.11
  76.0 1.4 %copy-start.10 = (f32[640]{0:T(1024)S(1)}, f32[640]{0:T(1024)}, u32[]{:S(2)}) copy-start(f32[640]{0:T(1024)} %get-tuple-element.52) | copy-start | bytes 7684
  76.8 1.2 %copy-start.8 = (f32[2560]{0:T(1024)S(1)}, f32[2560]{0:T(1024)}, u32[]{:S(2)}) copy-start(f32[2560]{0:T(1024)} %get-tuple-element.53) | copy-start | bytes 30724
  78.0 0.7 copy-start.9

commit v5 on v4

--- a/solution.py
+++ b/solution.py
@@ -403,6 +403,8 @@
 
     for d in (0, 1, 3):
         add_out(d, 0)
+    add_in(0)
+    add_out(2, 0)
     for copy in vzc:
         copy.wait_recv()
     total = vz[0]
@@ -410,17 +412,10 @@
         total = total + vz[q]
     vy[y] = total
     vyc = [send(vy.at[y], vy.at[y], vs.at[d], vr.at[d], to_y[d]) for d in (1, 3, 2)]
-    add_in(0)
-    add_out(2, 0)
     for d in (0, 1, 3):
         add_out(d, 1)
     add_in(1)
     add_out(2, 1)
-    for copy in vyc:
-        copy.wait_recv()
-    vx[x] = (vy[0] + vy[1]) + (vy[2] + vy[3])
-    vxc = [send(vx.at[x], vx.at[x], vs.at[3 + d], vr.at[3 + d], to_x[d]) for d in (1, 3, 2)]
-
     g3 = []
     for h, (cols, rows, groups) in enumerate(PARTS):
         for copy in g2[h]:
@@ -440,6 +435,10 @@
             send(zsend.at[zp[d], rows], r3.at[d - 1, rows], g3s.at[h, d - 1], g3r.at[h, d - 1], to_z[d])
             for d in (4, 3, 5, 2, 6, 1, 7)
         ]
+    for copy in vyc:
+        copy.wait_recv()
+    vx[x] = (vy[0] + vy[1]) + (vy[2] + vy[3])
+    vxc = [send(vx.at[x], vx.at[x], vs.at[3 + d], vr.at[3 + d], to_x[d]) for d in (1, 3, 2)]
     for copy in vxc:
         copy.wait_recv()
     total = ((vx[0] + vx[1]) + (vx[2] + vx[3])) * (1.0 / math.sqrt(TOKENS))

time: 79.5 us -> 77.5 us (0.975)
  Pallas kernels: 72.4 us -> 70.5 us
    pallas_call x1, Pallas kernels: 72.4 us -> 70.5 us  [body(): pl.pallas_call(kernel, out_shape=[jax.ShapeDtypeStruct(tokens.shape, BF)]...]
where the time goes in v5:
time: 77.5 us; the launch traced here: 77.3 us
  Pallas kernels  70.5 us (91%)
  local copies, waits for them, and re-layouts  4.48 us (6%)
  other arithmetic  1.56 us (2%)
    pallas_call x1, Pallas kernels, body(): pl.pallas_call(kernel, out_shape=[jax.ShapeDtypeStruct(tokens.shape, BF)]...  70.5 us
    unnamed x30, local copies, waits for them, and re-layouts  4.48 us
    sub x1, other arithmetic, adamw(): master - 0.001 * (new_moment / (jnp.sqrt(new_second) + 1e-08) + 0.1 * mas...  1.56 us

profile of v5, /device:TPU:8, one launch (start us, length us, event | category | flops | bytes accessed | tf_op | source)
XLA Modules:
  0.0 77.3 jit_solution(15914167248113955425)
XLA Ops:
  0.7 0.0 copy-start.2
  0.7 0.0 copy-start.3
  0.7 0.0 copy-start.4
  0.7 0.0 copy-start.5
  0.7 0.0 copy-start.6
  0.7 0.0 copy-start.7
  0.7 70.5 %shard_map.247 = (bf16[1,375,640]{2,1,0:T(8,128)(2,1)}, bf16[1,375,640]{2,1,0:T(8,128)(2,1)}, f32[640]{0:T(1024)}, f32[640]{0:T(1024)}, f32[2560]{0:T(1024)}, /*...) custom-call(bf16[1,375,640]{2,1,0:T(8,128)(2,1)} %tok_ref.1, bf16[1,375,640]{2,1,0:T(8,128)(2,1)} %cot_ref.1, ...), custom_call_target="tpu_custom_call" | custom-call | tf_op jit(solution)/shard_map/pallas_call | solution.py:476
  71.2 0.0 copy-start.1
  71.2 0.0 copy-done.2
  71.2 0.0 copy-done.3
  71.2 0.0 copy-done.4
  71.2 0.0 copy-done.5
  71.2 0.0 copy-done.6
  71.2 0.0 copy-done.7
  71.2 1.6 %multiply_subtract_fusion = (f32[10,640]{1,0:T(8,128)}, f32[10,640]{1,0:T(8,128)}, f32[10,640]{1,0:T(8,128)}, f32[10,640]{1,0:T(8,128)}, f32[10,640]{1,0:T(8,128)}, /*index=5*/f32[10,640]{1,0:T(8,128)}) fusion(f32[10,640]{1,0:T(8,128)S(1)} %copy-done.2, f32[10,640]{1,0:T(8,128)} %get-tuple-element.27, f32[10,640]{1,0:T(8,128)S(1)} %copy-done.3, ...), kind=kLoop, calls=%fused_computation | loop fusion | flops 179200 | bytes 358400 | tf_op jit(solution)/shard_map/sub | solution.py:110
  72.8 0.0 copy-done.1
  72.8 0.0 copy-start
  72.8 0.8 %copy.34 = bf16[1,375,640]{2,1,0:T(8,128)(2,1)} copy(bf16[1,375,640]{2,1,0:T(8,128)(2,1)S(1)} %copy-done.1) | data formatting | bytes 960000
  73.6 0.4 copy-done
  74.0 0.0 copy-start.11
  74.0 0.0 copy-start.10
  74.0 0.8 %copy.35 = bf16[1,375,640]{2,1,0:T(8,128)(2,1)} copy(bf16[1,375,640]{2,1,0:T(8,128)(2,1)S(1)} %copy-done) | data formatting | bytes 960000
  74.8 0.0 copy-done.11
  74.8 0.0 copy-start.8
  74.8 0.6 copy.36
  75.4 0.0 copy-done.10
  75.4 0.6 copy.37
  76.0 0.0 copy-done.8
  76.0 0.0 copy-start.9
  76.0 0.6 copy.38
  76.6 0.1 copy-done.9
  76.7 0.6 copy.39
Async XLA Ops:
  0.7 70.5 %copy-start.2 = (f32[10,640]{1,0:T(8,128)S(1)}, f32[10,640]{1,0:T(8,128)}, u32[]{:S(2)}) copy-start(f32[10,640]{1,0:T(8,128)} %param.29) | copy-start | bytes 76804
  0.7 70.5 %copy-start.3 = (f32[10,640]{1,0:T(8,128)S(1)}, f32[10,640]{1,0:T(8,128)}, u32[]{:S(2)}) copy-start(f32[10,640]{1,0:T(8,128)} %param.31) | copy-start | bytes 76804
  0.7 70.5 %copy-start.4 = (f32[10,640]{1,0:T(8,128)S(1)}, f32[10,640]{1,0:T(8,128)}, u32[]{:S(2)}) copy-start(f32[10,640]{1,0:T(8,128)} %param.30) | copy-start | bytes 76804
  0.7 70.5 %copy-start.5 = (f32[10,640]{1,0:T(8,128)S(1)}, f32[10,640]{1,0:T(8,128)}, u32[]{:S(2)}) copy-start(f32[10,640]{1,0:T(8,128)} %param.26) | copy-start | bytes 76804
  0.7 70.5 %copy-start.6 = (f32[10,640]{1,0:T(8,128)S(1)}, f32[10,640]{1,0:T(8,128)}, u32[]{:S(2)}) copy-start(f32[10,640]{1,0:T(8,128)} %param.28) | copy-start | bytes 76804
  0.7 70.5 %copy-start.7 = (f32[10,640]{1,0:T(8,128)S(1)}, f32[10,640]{1,0:T(8,128)}, u32[]{:S(2)}) copy-start(f32[10,640]{1,0:T(8,128)} %param.27) | copy-start | bytes 76804
  71.2 1.6 %copy-start.1 = (bf16[1,375,640]{2,1,0:T(8,128)(2,1)S(1)}, bf16[1,375,640]{2,1,0:T(8,128)(2,1)}, u32[]{:S(2)}) copy-start(bf16[1,375,640]{2,1,0:T(8,128)(2,1)} %get-tuple-element.49) | copy-start | bytes 1440004
  72.8 1.2 %copy-start = (bf16[1,375,640]{2,1,0:T(8,128)(2,1)S(1)}, bf16[1,375,640]{2,1,0:T(8,128)(2,1)}, u32[]{:S(2)}) copy-start(bf16[1,375,640]{2,1,0:T(8,128)(2,1)} %get-tuple-element.50) | copy-start | bytes 1440004
  74.0 0.8 %copy-start.11 = (f32[640]{0:T(1024)S(1)}, f32[640]{0:T(1024)}, u32[]{:S(2)}) copy-start(f32[640]{0:T(1024)} %get-tuple-element.51) | copy-start | bytes 7684
  74.0 1.4 %copy-start.10 = (f32[640]{0:T(1024)S(1)}, f32[640]{0:T(1024)}, u32[]{:S(2)}) copy-start(f32[640]{0:T(1024)} %get-tuple-element.52) | copy-start | bytes 7684
  74.8 1.2 %copy-start.8 = (f32[2560]{0:T(1024)S(1)}, f32[2560]{0:T(1024)}, u32[]{:S(2)}) copy-start(f32[2560]{0:T(1024)} %get-tuple-element.53) | copy-start | bytes 30724
  76.0 0.7 copy-start.9

commit v6 on v5

--- a/solution.py
+++ b/solution.py
@@ -405,6 +405,10 @@
         add_out(d, 0)
     add_in(0)
     add_out(2, 0)
+    for d in (0, 1, 3):
+        add_out(d, 1)
+    add_in(1)
+    add_out(2, 1)
     for copy in vzc:
         copy.wait_recv()
     total = vz[0]
@@ -412,10 +416,7 @@
         total = total + vz[q]
     vy[y] = total
     vyc = [send(vy.at[y], vy.at[y], vs.at[d], vr.at[d], to_y[d]) for d in (1, 3, 2)]
-    for d in (0, 1, 3):
-        add_out(d, 1)
-    add_in(1)
-    add_out(2, 1)
+
     g3 = []
     for h, (cols, rows, groups) in enumerate(PARTS):
         for copy in g2[h]:

time: 77.5 us -> 78.3 us (1.010)
  no operation moved by 1% of the time
where the time goes in v6:
time: 78.3 us; the launch traced here: 77.9 us
  Pallas kernels  71.1 us (91%)
  local copies, waits for them, and re-layouts  4.48 us (6%)
  other arithmetic  1.56 us (2%)
    pallas_call x1, Pallas kernels, body(): pl.pallas_call(kernel, out_shape=[jax.ShapeDtypeStruct(tokens.shape, BF)]...  71.1 us
    unnamed x30, local copies, waits for them, and re-layouts  4.48 us

profile of v6, /device:TPU:8, one launch (start us, length us, event | category | flops | bytes accessed | tf_op | source)
XLA Modules:
  0.0 77.9 jit_solution(18427003661533370714)
XLA Ops:
  0.7 0.0 copy-start.2
  0.7 0.0 copy-start.3
  0.7 0.0 copy-start.4
  0.7 0.0 copy-start.5
  0.7 0.0 copy-start.6
  0.7 0.0 copy-start.7
  0.7 71.1 %shard_map.247 = (bf16[1,375,640]{2,1,0:T(8,128)(2,1)}, bf16[1,375,640]{2,1,0:T(8,128)(2,1)}, f32[640]{0:T(1024)}, f32[640]{0:T(1024)}, f32[2560]{0:T(1024)}, /*...) custom-call(bf16[1,375,640]{2,1,0:T(8,128)(2,1)} %tok_ref.1, bf16[1,375,640]{2,1,0:T(8,128)(2,1)} %cot_ref.1, ...), custom_call_target="tpu_custom_call" | custom-call | tf_op jit(solution)/shard_map/pallas_call | solution.py:477
  71.8 0.0 copy-start.1
  71.8 0.0 copy-done.2
  71.8 0.0 copy-done.3
  71.8 0.0 copy-done.4
  71.8 0.0 copy-done.5
  71.8 0.0 copy-done.6
  71.8 0.0 copy-done.7
  71.8 1.6 %multiply_subtract_fusion = (f32[10,640]{1,0:T(8,128)}, f32[10,640]{1,0:T(8,128)}, f32[10,640]{1,0:T(8,128)}, f32[10,640]{1,0:T(8,128)}, f32[10,640]{1,0:T(8,128)}, /*index=5*/f32[10,640]{1,0:T(8,128)}) fusion(f32[10,640]{1,0:T(8,128)S(1)} %copy-done.2, f32[10,640]{1,0:T(8,128)} %get-tuple-element.27, f32[10,640]{1,0:T(8,128)S(1)} %copy-done.3, ...), kind=kLoop, calls=%fused_computation | loop fusion | flops 179200 | bytes 358400 | tf_op jit(solution)/shard_map/sub | solution.py:110
  73.4 0.0 copy-done.1
  73.4 0.0 copy-start
  73.4 0.8 copy.34
  74.2 0.4 copy-done
  74.6 0.0 copy-start.11
  74.6 0.0 copy-start.10
  74.6 0.8 copy.35
  75.4 0.0 copy-done.11
  75.4 0.0 copy-start.8
  75.4 0.6 copy.36
  76.0 0.0 copy-done.10
  76.0 0.6 copy.37
  76.6 0.0 copy-done.8
  76.6 0.0 copy-start.9
  76.6 0.6 copy.38
  77.2 0.1 copy-done.9
  77.3 0.6 copy.39
Async XLA Ops:
  0.7 71.1 %copy-start.2 = (f32[10,640]{1,0:T(8,128)S(1)}, f32[10,640]{1,0:T(8,128)}, u32[]{:S(2)}) copy-start(f32[10,640]{1,0:T(8,128)} %param.29) | copy-start | bytes 76804
  0.7 71.1 %copy-start.3 = (f32[10,640]{1,0:T(8,128)S(1)}, f32[10,640]{1,0:T(8,128)}, u32[]{:S(2)}) copy-start(f32[10,640]{1,0:T(8,128)} %param.31) | copy-start | bytes 76804
  0.7 71.1 %copy-start.4 = (f32[10,640]{1,0:T(8,128)S(1)}, f32[10,640]{1,0:T(8,128)}, u32[]{:S(2)}) copy-start(f32[10,640]{1,0:T(8,128)} %param.30) | copy-start | bytes 76804
  0.7 71.1 %copy-start.5 = (f32[10,640]{1,0:T(8,128)S(1)}, f32[10,640]{1,0:T(8,128)}, u32[]{:S(2)}) copy-start(f32[10,640]{1,0:T(8,128)} %param.26) | copy-start | bytes 76804
  0.7 71.1 %copy-start.6 = (f32[10,640]{1,0:T(8,128)S(1)}, f32[10,640]{1,0:T(8,128)}, u32[]{:S(2)}) copy-start(f32[10,640]{1,0:T(8,128)} %param.28) | copy-start | bytes 76804
  0.7 71.1 %copy-start.7 = (f32[10,640]{1,0:T(8,128)S(1)}, f32[10,640]{1,0:T(8,128)}, u32[]{:S(2)}) copy-start(f32[10,640]{1,0:T(8,128)} %param.27) | copy-start | bytes 76804
  71.8 1.6 %copy-start.1 = (bf16[1,375,640]{2,1,0:T(8,128)(2,1)S(1)}, bf16[1,375,640]{2,1,0:T(8,128)(2,1)}, u32[]{:S(2)}) copy-start(bf16[1,375,640]{2,1,0:T(8,128)(2,1)} %get-tuple-element.49) | copy-start | bytes 1440004
  73.4 1.2 %copy-start = (bf16[1,375,640]{2,1,0:T(8,128)(2,1)S(1)}, bf16[1,375,640]{2,1,0:T(8,128)(2,1)}, u32[]{:S(2)}) copy-start(bf16[1,375,640]{2,1,0:T(8,128)(2,1)} %get-tuple-element.50) | copy-start | bytes 1440004
  74.6 0.8 %copy-start.11 = (f32[640]{0:T(1024)S(1)}, f32[640]{0:T(1024)}, u32[]{:S(2)}) copy-start(f32[640]{0:T(1024)} %get-tuple-element.51) | copy-start | bytes 7684
  74.6 1.4 %copy-start.10 = (f32[640]{0:T(1024)S(1)}, f32[640]{0:T(1024)}, u32[]{:S(2)}) copy-start(f32[640]{0:T(1024)} %get-tuple-element.52) | copy-start | bytes 7684
  75.4 1.2 %copy-start.8 = (f32[2560]{0:T(1024)S(1)}, f32[2560]{0:T(1024)}, u32[]{:S(2)}) copy-start(f32[2560]{0:T(1024)} %get-tuple-element.53) | copy-start | bytes 30724
  76.6 0.7 copy-start.9
